TPU v7x, 512 devices: a whole 4x8x8 slice. The times are simulated.
512 devices in a mesh: rep: 64 (over z, y_hi, core), fsdp: 8 (over x, y_lo).
Axes of the slice: x: 4, y: 8 (y_hi: 4, y_lo: 2; y = y_hi * 2 + y_lo), z: 8, core: 2. Of those that a mesh axis runs over, the one named last changes fastest.
Arguments:
- hidden: bfloat16 [2, 65536, 4096], P(None, ('rep', 'fsdp')), may hold values from -6 to 6
- cotangent: bfloat16 [2, 65536, 512], P(None, ('rep', 'fsdp')), may hold values from -6 to 6
- local_weight: bfloat16 [64, 512, 4096], P('rep', None, 'fsdp'), may hold values from -16 to 16
- first_moment: bfloat16 [64, 512, 4096], P('rep', None, 'fsdp'), may hold values from -1.5 to 1.5
- second_moment: bfloat16 [64, 512, 4096], P('rep', None, 'fsdp'), may hold values from 0.0099487305 to 0.29882812
- global_weight: float32 [512, 4096], P('rep', 'fsdp'), may hold values from -6 to 6
- outer_momentum: float32 [512, 4096], P('rep', 'fsdp'), may hold values from -4 to 4
- step_count: int32 [1], replicated, may hold values from 1 to 5
Outputs:
- projected_keys: bfloat16 [2, 65536, 512], P(None, ('rep', 'fsdp'))
- final_weight: bfloat16 [64, 512, 4096], P('rep', None, 'fsdp')
- new_global: float32 [512, 4096], P('rep', 'fsdp')
- new_momentum: float32 [512, 4096], P('rep', 'fsdp')
All inputs are finite; a program needn't handle non-finite values.
Results may differ from a plain program's by a relative error of at most 0.001.
The roundings to bfloat16 on the way count: a program that leaves them out, or rounds other values in their place, can miss the bound.
Values may be sent and summed in bfloat16 or wider, within the bound.
No kernel may reach another device: no remote copies, remote signals or barrier semaphores. Data moves between devices by JAX's collectives and lax.ppermute only.
A program may use at most 64 MiB of HBM per device.

v0:
```python
import jax
import jax.numpy as jnp
from jax import lax
from jax.sharding import PartitionSpec as P

D = 4096
STEPS = 2


def outer_update(local_weight, global_weight, outer_momentum):
    replica_count = lax.axis_size("rep")
    widened = local_weight[0].astype(jnp.float32)
    summed = lax.psum(widened, "rep")
    share_rows = global_weight.shape[0]
    summed = lax.dynamic_slice_in_dim(summed, lax.axis_index("rep") * share_rows, share_rows, 0)
    difference = global_weight - summed / replica_count
    momentum = 0.9 * outer_momentum + difference
    updated = global_weight - 0.7 * (difference + 0.9 * momentum)
    landed = lax.all_gather(updated, "rep", axis=0, tiled=True)
    return (updated, momentum, landed)


def per_device(
    hidden,
    cotangent,
    local_weight,
    first_moment,
    second_moment,
    global_weight,
    outer_momentum,
    step_count,
):
    factor = D ** (-0.5)
    columns = lax.all_to_all(hidden, "fsdp", split_axis=2, concat_axis=1, tiled=True)
    cotangents = lax.all_gather(cotangent, "fsdp", axis=1, tiled=True)
    weight = local_weight[0].astype(jnp.float32)
    moment_one = first_moment[0].astype(jnp.float32)
    moment_two = second_moment[0].astype(jnp.float32)
    first_count = step_count[0].astype(jnp.float32)
    landed_state = None
    key_list = []
    for inner in range(STEPS):
        weight_bf = weight.astype(jnp.bfloat16)
        step_columns = columns[inner]
        step_upstream = cotangents[inner]
        product = lax.dot_general(
            step_columns, weight_bf, (((1,), (1,)), ((), ())), preferred_element_type=jnp.float32
        )
        key_rows = lax.psum_scatter(product * factor, "fsdp", scatter_dimension=0, tiled=True)
        key_list.append(key_rows.astype(jnp.bfloat16))
        gradient = (
            lax.dot_general(
                step_upstream,
                step_columns,
                (((0,), (0,)), ((), ())),
                preferred_element_type=jnp.float32,
            )
            * factor
        )
        moment_one = 0.9 * moment_one + 0.1 * gradient
        moment_two = 0.95 * moment_two + 0.05 * gradient * gradient
        counter = first_count + (inner + 1)
        bias_one = 1.0 - jnp.power(0.9, counter)
        bias_two = 1.0 - jnp.power(0.95, counter)
        weight = weight - 0.05 * (
            moment_one / bias_one / (jnp.sqrt(moment_two / bias_two) + 1e-08) + 0.1 * weight
        )
        if inner == 0:
            landed_state = outer_update(local_weight, global_weight, outer_momentum)
            weight = 0.5 * weight + 0.5 * landed_state[2]
    projected_keys = jnp.stack(key_list)
    final_weight = weight.astype(jnp.bfloat16)[None]
    return (projected_keys, final_weight, landed_state[0], landed_state[1])


def solution(mesh):
    placed = (
        P(None, ("rep", "fsdp"), None),
        P(None, ("rep", "fsdp"), None),
        P("rep", None, "fsdp"),
        P("rep", None, "fsdp"),
        P("rep", None, "fsdp"),
        P("rep", "fsdp"),
        P("rep", "fsdp"),
        P(),
    )
    return jax.shard_map(
        per_device,
        mesh=mesh,
        in_specs=placed,
        out_specs=(
            P(None, ("rep", "fsdp"), None),
            P("rep", None, "fsdp"),
            P("rep", "fsdp"),
            P("rep", "fsdp"),
        ),
        check_vma=False,
    )
```

profile of v0, /device:TPU:1, one launch (start us, length us, event | category | flops | bytes accessed | tf_op | source)
XLA Modules:
  0.0 810.2 jit_solution(7403381852805417353)
XLA Ops:
  8.0 0.0 copy-start.1
  8.0 0.0 all-reduce.2.cloned.1.call-start
  8.1 2.3 bitcast_convert_fusion
  10.4 0.0 all-reduce.2.cloned.1.call-update
  10.4 0.0 all-gather.3.cloned.1.call-start
  10.5 0.5 all-gather.3.cloned.1.call-update
  11.0 0.0 copy-done.1
  11.0 3.8 copy.18
  14.8 0.0 copy-start.2
  14.8 0.0 copy-start.3
  14.8 6.0 all-to-all-start
  20.8 0.0 all-gather.5.cloned.1.call-start
  20.8 580.7 %all-reduce.2.cloned.1.call-done = f32[512,512]{1,0:T(8,128)} async-done(((f32[512,512]{1,0:T(8,128)}), f32[512,512]{1,0:T(8,128)}) %all-reduce.2.cloned.1.call-update) | async-done | bytes 1048592 | tf_op jit(solution)/shard_map/psum | solution.py:13
  601.5 0.0 copy-done.2
  601.5 0.0 copy-done.3
  601.5 1.3 multiply_subtract_fusion
  602.8 0.0 all-gather.5.cloned.1.call-update
  602.9 0.0 reduce-scatter.5.cloned.1.call-start
  603.7 0.0 all-to-all-done
  603.7 0.3 copy.19
  603.9 0.1 fusion.6
  604.1 0.5 copy.20
  604.6 0.5 copy.21
  605.2 0.0 all-gather.3.cloned.1.call-done
  605.2 0.0 copy-start
  605.2 0.0 copy-start.5
  605.2 3.1 fusion.1
  608.3 74.5 %all-gather.5.cloned.1.call-done = f32[512,512]{1,0:T(8,128)} async-done(((f32[8,512]{1,0:T(8,128)}), f32[512,512]{1,0:T(8,128)}) %all-gather.5.cloned.1.call-update) | async-done | bytes 1048592 | tf_op jit(solution)/shard_map/all_gather | solution.py:19
  682.8 0.0 copy-done
  682.8 0.0 copy-done.5
  682.8 4.5 multiply_bitcast_fusion
  687.3 0.0 reduce-scatter.5.cloned.1.call-update
  687.4 0.0 reduce-scatter.3.cloned.1.call-start
  687.4 2.1 convolution_multiply_fusion
  689.5 0.0 copy-start.4
  689.5 0.0 reduce-scatter.3.cloned.1.call-update
  689.6 1.1 copy-done.4
  690.7 4.8 fusion.2
  695.6 45.2 %reduce-scatter.5.cloned.1.call-done = f32[128,512]{1,0:T(8,128)} async-done(((f32[1024,512]{1,0:T(8,128)}), f32[128,512]{1,0:T(8,128)}) %reduce-scatter.5.cloned.1.call-update) | async-done | bytes 262160 | tf_op jit(solution)/shard_map/reduce_scatter | solution.py:49
  740.7 1.0 convert_bitcast_fusion
  741.7 59.2 %reduce-scatter.3.cloned.1.call-done = f32[128,512]{1,0:T(8,128)} async-done(((f32[1024,512]{1,0:T(8,128)}), f32[128,512]{1,0:T(8,128)}) %reduce-scatter.3.cloned.1.call-update) | async-done | bytes 262160 | tf_op jit(solution)/shard_map/reduce_scatter | solution.py:49
  800.9 1.0 convert_bitcast_fusion.1
  801.8 0.7 pad_maximum_fusion
Async XLA Ops:
  8.0 3.0 copy-start.1
  8.0 593.5 %all-reduce.2.cloned.1.call-start = ((), (), s32[]{:S(2)}) async-start(), calls=%async_computation.5 | async-start | bytes 2097152 | tf_op jit(solution)/shard_map/psum | solution.py:13
  10.4 594.8 %all-gather.3.cloned.1.call-start = ((), (), s32[]{:S(2)}) async-start(), calls=%async_computation.4 | async-start | bytes 2359296 | tf_op jit(solution)/shard_map/all_gather | solution.py:35
  14.8 586.7 %copy-start.2 = (f32[8,512]{1,0:T(8,128)S(1)}, f32[8,512]{1,0:T(8,128)}, u32[]{:S(2)}) copy-start(f32[8,512]{1,0:T(8,128)} %param.13) | copy-start | bytes 49156
  14.8 586.7 %copy-start.3 = (f32[8,512]{1,0:T(8,128)S(1)}, f32[8,512]{1,0:T(8,128)}, u32[]{:S(2)}) copy-start(f32[8,512]{1,0:T(8,128)} %param.14) | copy-start | bytes 49156
  14.8 588.9 %all-to-all-start = ((bf16[2,128,4096]{1,0,2:T(2,128)(2,1)}), bf16[2,128,4096]{1,0,2:T(2,128)(2,1)S(1)}, u32[]{:S(2)}, u32[]{:S(2)}) async-start(bf16[2,128,4096]{1,0,2:T(2,128)(2,1)} %copy.18), calls=%async_computation | async-start | bytes 4194304 | tf_op jit(solution)/shard_map/all_to_all | solution.py:34
  20.8 662.0 %all-gather.5.cloned.1.call-start = ((), (), s32[]{:S(2)}) async-start(), calls=%async_computation.6 | async-start | bytes 1064960 | tf_op jit(solution)/shard_map/all_gather | solution.py:19
  602.9 137.9 %reduce-scatter.5.cloned.1.call-start = ((), (), s32[]{:S(2)}) async-start(), calls=%async_computation.7 | async-start | bytes 2359296 | tf_op jit(solution)/shard_map/reduce_scatter | solution.py:49
  605.2 77.6 %copy-start = (bf16[1,512,512]{2,1,0:T(8,128)(2,1)S(1)}, bf16[1,512,512]{2,1,0:T(8,128)(2,1)}, u32[]{:S(2)}) copy-start(bf16[1,512,512]{2,1,0:T(8,128)(2,1)} %param.10) | copy-start | bytes 1572868
  605.2 77.6 %copy-start.5 = (bf16[1,512,512]{2,1,0:T(8,128)(2,1)S(1)}, bf16[1,512,512]{2,1,0:T(8,128)(2,1)}, u32[]{:S(2)}) copy-start(bf16[1,512,512]{2,1,0:T(8,128)(2,1)} %param.11) | copy-start | bytes 1572868
  687.4 113.5 %reduce-scatter.3.cloned.1.call-start = ((), (), s32[]{:S(2)}) async-start(), calls=%async_computation.3 | async-start | bytes 2359296 | tf_op jit(solution)/shard_map/reduce_scatter | solution.py:49
  689.5 1.2 copy-start.4
Sparse Core Ops, SparseCore 0:
  11.7 589.7 all-reduce.1
Sparse Core Ops, SparseCore 1:
  13.0 74.9 all-gather.2
  603.0 79.8 all-gather.4
  687.4 53.2 reduce-scatter.4
  743.8 57.0 reduce-scatter.2
where the time goes:
time: 811 us; the launch traced here: 810 us
  waiting for transfers between devices  760 us (94%)
  between operations  16.6 us (2%)
  matrix products  14.5 us (2%)
    psum x1, waiting for transfers between devices, outer_update(): summed = lax.psum(widened, 'rep')  581 us
    reduce_scatter x2, waiting for transfers between devices, per_device(): lax.psum_scatter(product * factor, 'fsdp', scatter_dimension=0, tiled=True)  104 us
    all_gather x1, waiting for transfers between devices, outer_update(): landed = lax.all_gather(updated, 'rep', axis=0, tiled=True)  74.5 us
  transfers between devices with their start and end apart: 6, of which 4 were waited for; matrix products, arithmetic and copies ran while one was open for 2% of the time, Pallas kernels for 0%

commit v1 on v0

v1 whole, which is shorter than its diff:
```python
import jax
import jax.numpy as jnp
from jax import lax
from jax.sharding import Mesh, PartitionSpec as P

D = 4096
STEPS = 2
REP = ("z", "y_hi", "core")
COLUMN = ("z", "y_hi")
FSDP = ("x", "y_lo")


def outer_update(local_weight, global_weight, outer_momentum):
    replicas = lax.axis_size(REP)
    rows, width = global_weight.shape
    shares = lax.all_to_all(
        local_weight[0].reshape(replicas, rows, width), REP, 0, 0, tiled=True
    )
    mean_local = jnp.sum(shares.astype(jnp.float32), axis=0) / replicas
    difference = global_weight - mean_local
    momentum = 0.9 * outer_momentum + difference
    updated = global_weight - 0.7 * (difference + 0.9 * momentum)
    columns = lax.axis_size(COLUMN)
    mine = lax.all_to_all(
        jnp.broadcast_to(updated, (columns, rows, width)), COLUMN, 0, 0, tiled=True
    )
    other = lax.ppermute(mine, "core", [(0, 1), (1, 0)])
    first = lax.axis_index("core") == 0
    landed = jnp.stack(
        [jnp.where(first, mine, other), jnp.where(first, other, mine)], axis=1
    ).reshape(replicas * rows, width)
    return (updated, momentum, landed)


def keys_by_exchange(product):
    parts = lax.axis_size(FSDP)
    rows, width = product.shape
    pieces = lax.all_to_all(
        product.reshape(parts, rows // parts, width), FSDP, 0, 0, tiled=True
    )
    return jnp.sum(pieces, axis=0)


def per_device(
    hidden,
    cotangent,
    local_weight,
    first_moment,
    second_moment,
    global_weight,
    outer_momentum,
    step_count,
):
    factor = D ** (-0.5)
    parts = lax.axis_size(FSDP)
    tokens = hidden.shape[1]
    width = hidden.shape[2] // parts
    cotangents = lax.all_gather(cotangent, FSDP, axis=1, tiled=True)
    updated, momentum, landed = outer_update(local_weight, global_weight, outer_momentum)
    by_owner = hidden.reshape(STEPS, tokens, parts, width).transpose(2, 0, 1, 3)
    columns = lax.all_to_all(by_owner, FSDP, 0, 0, tiled=True)
    weight = local_weight[0].astype(jnp.float32)
    moment_one = first_moment[0].astype(jnp.float32)
    moment_two = second_moment[0].astype(jnp.float32)
    first_count = step_count[0].astype(jnp.float32)
    key_list = []
    for inner in range(STEPS):
        weight_bf = weight.astype(jnp.bfloat16)
        step_columns = columns[:, inner].reshape(parts * tokens, width)
        step_upstream = cotangents[inner]
        product = lax.dot_general(
            step_columns, weight_bf, (((1,), (1,)), ((), ())), preferred_element_type=jnp.float32
        )
        if inner == 0:
            key_rows = lax.psum_scatter(product, FSDP, scatter_dimension=0, tiled=True)
        else:
            key_rows = keys_by_exchange(product)
        key_list.append((key_rows * factor).astype(jnp.bfloat16))
        gradient = (
            lax.dot_general(
                step_upstream,
                step_columns,
                (((0,), (0,)), ((), ())),
                preferred_element_type=jnp.float32,
            )
            * factor
        )
        moment_one = 0.9 * moment_one + 0.1 * gradient
        moment_two = 0.95 * moment_two + 0.05 * gradient * gradient
        counter = first_count + (inner + 1)
        bias_one = 1.0 - jnp.power(0.9, counter)
        bias_two = 1.0 - jnp.power(0.95, counter)
        weight = weight - 0.05 * (
            moment_one / bias_one / (jnp.sqrt(moment_two / bias_two) + 1e-08) + 0.1 * weight
        )
        if inner == 0:
            weight = 0.5 * weight + 0.5 * landed
    projected_keys = jnp.stack(key_list)
    final_weight = weight.astype(jnp.bfloat16)[None]
    return (projected_keys, final_weight, updated, momentum)


def solution(mesh):
    chips = Mesh(mesh.devices.reshape(8, 4, 2, 4, 2), REP + FSDP)
    tokens = P(None, REP + FSDP, None)
    replica = P(REP, None, FSDP)
    outer = P(REP, FSDP)
    return jax.shard_map(
        per_device,
        mesh=chips,
        in_specs=(tokens, tokens, replica, replica, replica, outer, outer, P()),
        out_specs=(tokens, replica, outer, outer),
        check_vma=False,
    )
```

time: 811 us -> 229 us (0.28)
  waiting for transfers between devices: 760 us -> 131 us
  blocking collectives: 0 us -> 38.4 us
  starting transfers between devices: 6.2 us -> 16 us
    psum x1 -> x0, waiting for transfers between devices: 581 us -> none  [outer_update(): summed = lax.psum(widened, 'rep')]
    reduce_scatter x2 -> x1, waiting for transfers between devices: 104 us -> 15.5 us  [per_device(): key_rows = lax.psum_scatter(product, FSDP, scatter_dimension=0, tiled=True)]
    all_to_all x1 -> x3, waiting for transfers between devices: 0.01 us -> 84.6 us  [the longest x1 44.6 us: keys_by_exchange(): lax.all_to_all(product.reshape(parts, rows // parts, width), FSDP, 0, 0,...]
    all_gather x2 -> x1, waiting for transfers between devices: 74.5 us -> 29.9 us  [per_device(): cotangents = lax.all_gather(cotangent, FSDP, axis=1, tiled=True)]
    all_to_all x0 -> x1, blocking collectives: none -> 38.4 us  [outer_update(): lax.all_to_all(local_weight[0].reshape(replicas, rows, width), REP, 0, 0,...]
  transfers between devices with their start and end apart: 6 -> 6, of which waited for: 4 -> 6; matrix products, arithmetic and copies ran while one was open for 2% -> 10% of each run, Pallas kernels for 0% -> 0%
where the time goes in v1:
time: 229 us; the launch traced here: 228 us
  waiting for transfers between devices  131 us (57%)
  blocking collectives  38.4 us (17%)
  starting transfers between devices  16 us (7%)
  between operations  15 us (7%)
  matrix products  12.1 us (5%)
  local copies, waits for them, and re-layouts  10.5 us (5%)
  other arithmetic  4.45 us (2%)
    all_to_all x1, waiting for transfers between devices, keys_by_exchange(): lax.all_to_all(product.reshape(parts, rows // parts, width), FSDP, 0, 0,...  44.6 us
    all_to_all x1, blocking collectives, outer_update(): lax.all_to_all(local_weight[0].reshape(replicas, rows, width), REP, 0, 0,...  38.4 us
    all_gather x1, waiting for transfers between devices, per_device(): cotangents = lax.all_gather(cotangent, FSDP, axis=1, tiled=True)  29.9 us
    all_to_all x1, waiting for transfers between devices, per_device(): columns = lax.all_to_all(by_owner, FSDP, 0, 0, tiled=True)  25.1 us
    reduce_scatter x1, waiting for transfers between devices, per_device(): key_rows = lax.psum_scatter(product, FSDP, scatter_dimension=0, tiled=True)  15.5 us
    all_to_all x1, waiting for transfers between devices, outer_update(): lax.all_to_all(jnp.broadcast_to(updated, (columns, rows, width)), COLUMN,...  14.8 us
    dot_general x2, matrix products, per_device(): lax.dot_general(step_upstream, step_columns, (((0,), (0,)), ((), ())), pr...  9.29 us
    unnamed x15, local copies, waits for them, and re-layouts  5.41 us
  transfers between devices with their start and end apart: 6, of which 6 were waited for; matrix products, arithmetic and copies ran while one was open for 10% of the time, Pallas kernels for 0%

profile of v1, /device:TPU:1, one launch (start us, length us, event | category | flops | bytes accessed | tf_op | source)
XLA Modules:
  0.0 227.8 jit_solution(5033353614963339818)
XLA Ops:
  7.2 38.4 %all_to_all.20 = bf16[64,8,512]{2,1,0:T(8,128)(2,1)S(1)} all-to-all(bf16[64,8,512]{2,1,0:T(8,128)(2,1)} %bitcast.68), channel_id=1, replica_groups=mesh['z'=8,'y_hi'=4,'core'=2,'x'=4,'y_lo'=2] {'z','y_hi','core'}, dimensions={0} | all-to-all | bytes 1048576 | tf_op jit(solution)/shard_map/all_to_all | solution.py:16
  45.6 0.1 convert_reduce_fusion
  45.7 1.3 multiply_subtract_fusion
  47.0 0.0 copy-start.4
  47.0 0.9 broadcast_in_dim.6
  47.9 4.4 %all-to-all-start.2 = ((f32[32,8,512]{2,1,0:T(8,128)}), f32[32,8,512]{2,1,0:T(8,128)S(1)}, u32[]{:S(2)}, u32[]{:S(2)}) async-start(f32[32,8,512]{2,1,0:T(8,128)} %broadcast_in_dim.6), calls=%async_computation.3 | async-start | bytes 1048576 | tf_op jit(solution)/shard_map/all_to_all | solution.py:24
  52.3 3.1 %copy.18 = bf16[2,128,4096]{1,2,0:T(8,128)(2,1)S(1)} copy(bf16[2,128,4096]{2,1,0:T(8,128)(2,1)} %param.8) | data formatting | bytes 4194304 | tf_op args[0]
  55.4 0.0 copy-done.4
  55.4 1.5 copy.19
  56.9 14.8 %all-to-all-done.2 = f32[32,8,512]{2,1,0:T(8,128)S(1)} async-done(((f32[32,8,512]{2,1,0:T(8,128)}), f32[32,8,512]{2,1,0:T(8,128)S(1)}, u32[]{:S(2)}, u32[]{:S(2)}) %all-to-all-start.2) | async-done | bytes 524320 | tf_op jit(solution)/shard_map/all_to_all | solution.py:24
  71.7 4.0 %all-to-all-start = ((bf16[8,2,128,512]{2,3,1,0:T(8,128)(2,1)}), bf16[8,2,128,512]{2,3,1,0:T(8,128)(2,1)S(1)}, u32[]{:S(2)}, u32[]{:S(2)}) async-start(bf16[8,2,128,512]{2,3,1,0:T(8,128)(2,1)} %copy.19), calls=%async_computation | async-start | bytes 4194304 | tf_op jit(solution)/shard_map/all_to_all | solution.py:61
  75.8 0.0 all-gather.2.cloned.1.call-start
  75.8 0.7 all-gather.2.cloned.1.call-update
  76.5 0.0 reduce-scatter.2.cloned.1.call-start
  76.5 3.8 %collective-permute-start = (f32[32,8,512]{2,1,0:T(8,128)S(1)}, f32[32,8,512]{2,1,0:T(8,128)S(1)}, u32[]{:S(2)}, u32[]{:S(2)}) collective-permute-start(f32[32,8,512]{2,1,0:T(8,128)S(1)} %all-to-all-done.2), channel_id=1, source_target_pairs={{0,8},{8,0},{1,9},{9,1},{2,10},{10,2},{3,11},{11,3},{4,12},{12,4},... | collective-permute-start | bytes 1572872 | tf_op jit(solution)/shard_map/ppermute | solution.py:27
  81.1 0.8 collective-permute-done
  81.9 0.1 select_bitcast_fusion.1
  82.0 1.1 pad_maximum_fusion
  83.1 25.1 %all-to-all-done = bf16[8,2,128,512]{2,3,1,0:T(8,128)(2,1)S(1)} async-done(((bf16[8,2,128,512]{2,3,1,0:T(8,128)(2,1)}), bf16[8,2,128,512]{2,3,1,0:T(8,128)(2,1)S(1)}, u32[]{:S(2)}, u32[]{:S(2)}) %all-to-all-start) | async-done | bytes 2097184 | tf_op jit(solution)/shard_map/all_to_all | solution.py:61
  108.2 1.2 fusion.12
  109.4 0.0 copy-start.1
  109.4 0.5 copy.27
  109.9 0.5 copy-done.1
  110.4 0.0 copy-start.2
  110.4 0.0 copy-start.5
  110.4 2.1 fusion.6
  112.5 0.0 reduce-scatter.2.cloned.1.call-update
  112.6 29.9 %all-gather.2.cloned.1.call-done = bf16[2,1024,512]{2,1,0:T(8,128)(2,1)} async-done(((bf16[2,128,512]{2,1,0:T(8,128)(2,1)}), bf16[2,1024,512]{2,1,0:T(8,128)(2,1)}) %all-gather.2.cloned.1.call-update) | async-done | bytes 2097168 | tf_op jit(solution)/shard_map/all_gather | solution.py:58
  142.5 0.0 copy-done.2
  142.5 0.0 copy-done.5
  142.5 0.0 copy-start
  142.5 4.6 %fusion.2 = (f32[512,512]{1,0:T(8,128)}, f32[512,512]{1,0:T(8,128)}) fusion(f32[32,2,8,512]{3,2,1,0:T(8,128)} %pad_maximum_fusion, bf16[1,512,512]{2,1,0:T(8,128)(2,1)S(1)} %copy-done.5, bf16[1,512,512]{2,1,0:T(8,128)(2,1)S(1)} %copy-done.2, f32[]{:T(128)} %bitcast.9, bf16[1,512,512]{2,1,0:T(8,128)(2,1)} %param.12, f32[]{:T(128)} %bitcast.7, ...), kind=kOutput, calls=%fused_computation.6 | convolution fusion | flops 542113792 | bytes 6816768 | tf_op jit(solution)/shard_map/dot_general | solution.py:80
  147.1 0.0 copy-start.3
  147.1 0.0 copy-done
  147.1 0.5 copy.28
  147.6 0.7 copy-done.3
  148.3 0.7 convolution_bitcast_fusion
  149.0 1.5 copy.31
  150.5 3.6 %all-to-all-start.3 = ((f32[8,128,512]{1,2,0:T(8,128)}), f32[8,128,512]{1,2,0:T(8,128)S(1)}, u32[]{:S(2)}, u32[]{:S(2)}) async-start(f32[8,128,512]{1,2,0:T(8,128)} %bitcast.62), calls=%async_computation.4 | async-start | bytes 4194304 | tf_op jit(solution)/shard_map/all_to_all | solution.py:38
  154.2 4.7 %fusion.5 = bf16[1,512,512]{2,1,0:T(8,128)(2,1)} fusion(f32[512,512]{1,0:T(8,128)} %get-tuple-element.10, bf16[1024,512]{1,0:T(8,128)(2,1)S(1)} %bitcast.67, bf16[2,1024,512]{2,1,0:T(8,128)(2,1)} %all-gather.2.cloned.1.call-done, f32[512,512]{1,0:T(8,128)} %get-tuple-element.11, bf16[1,512,512]{2,1,0:T(8,128)(2,1)} %param.11, f32[]{:T(128)} %bitcast.20, ...), kind=kOutput, calls=%fused_computation.16 | convolution fusion | flops 544210944 | bytes 5768192 | tf_op jit(solution)/shard_map/dot_general | solution.py:80
  158.9 44.6 %all-to-all-done.3 = f32[8,128,512]{1,2,0:T(8,128)S(1)} async-done(((f32[8,128,512]{1,2,0:T(8,128)}), f32[8,128,512]{1,2,0:T(8,128)S(1)}, u32[]{:S(2)}, u32[]{:S(2)}) %all-to-all-start.3) | async-done | bytes 2097184 | tf_op jit(solution)/shard_map/all_to_all | solution.py:38
  203.6 0.1 reduce_sum.19
  203.7 0.1 copy.25
  203.8 15.5 %reduce-scatter.2.cloned.1.call-done = f32[128,512]{1,0:T(8,128)} async-done(((f32[1024,512]{1,0:T(8,128)}), f32[128,512]{1,0:T(8,128)}) %reduce-scatter.2.cloned.1.call-update) | async-done | bytes 262160 | tf_op jit(solution)/shard_map/reduce_scatter | solution.py:75
  219.3 1.0 fusion.9
  220.3 0.7 pad_maximum_fusion.1
  (1 shorter events, 0.0 us)
Async XLA Ops:
  47.0 8.4 %copy-start.4 = (f32[8,512]{1,0:T(8,128)}, f32[8,512]{1,0:T(8,128)S(1)}, u32[]{:S(2)}) copy-start(f32[8,512]{1,0:T(8,128)S(1)} %get-tuple-element.4) | copy-start | bytes 49156
  47.9 23.9 %all-to-all-start.2 = ((f32[32,8,512]{2,1,0:T(8,128)}), f32[32,8,512]{2,1,0:T(8,128)S(1)}, u32[]{:S(2)}, u32[]{:S(2)}) async-start(f32[32,8,512]{2,1,0:T(8,128)} %broadcast_in_dim.6), calls=%async_computation.3 | async-start | bytes 1048576 | tf_op jit(solution)/shard_map/all_to_all | solution.py:24
  71.7 36.5 %all-to-all-start = ((bf16[8,2,128,512]{2,3,1,0:T(8,128)(2,1)}), bf16[8,2,128,512]{2,3,1,0:T(8,128)(2,1)S(1)}, u32[]{:S(2)}, u32[]{:S(2)}) async-start(bf16[8,2,128,512]{2,3,1,0:T(8,128)(2,1)} %copy.19), calls=%async_computation | async-start | bytes 4194304 | tf_op jit(solution)/shard_map/all_to_all | solution.py:61
  75.8 66.7 %all-gather.2.cloned.1.call-start = ((), (), s32[]{:S(2)}) async-start(), calls=%async_computation.6 | async-start | bytes 2359296 | tf_op jit(solution)/shard_map/all_gather | solution.py:58
  76.5 142.8 %reduce-scatter.2.cloned.1.call-start = ((), (), s32[]{:S(2)}) async-start(), calls=%async_computation.5 | async-start | bytes 2359296 | tf_op jit(solution)/shard_map/reduce_scatter | solution.py:75
  76.5 5.4 %collective-permute-start = (f32[32,8,512]{2,1,0:T(8,128)S(1)}, f32[32,8,512]{2,1,0:T(8,128)S(1)}, u32[]{:S(2)}, u32[]{:S(2)}) collective-permute-start(f32[32,8,512]{2,1,0:T(8,128)S(1)} %all-to-all-done.2), channel_id=1, source_target_pairs={{0,8},{8,0},{1,9},{9,1},{2,10},{10,2},{3,11},{11,3},{4,12},{12,4},... | collective-permute-start | bytes 1572872 | tf_op jit(solution)/shard_map/ppermute | solution.py:27
  109.4 1.0 copy-start.1
  110.4 32.0 %copy-start.2 = (bf16[1,512,512]{2,1,0:T(8,128)(2,1)S(1)}, bf16[1,512,512]{2,1,0:T(8,128)(2,1)}, u32[]{:S(2)}) copy-start(bf16[1,512,512]{2,1,0:T(8,128)(2,1)} %param.10) | copy-start | bytes 1572868
  110.4 32.0 %copy-start.5 = (bf16[1,512,512]{2,1,0:T(8,128)(2,1)S(1)}, bf16[1,512,512]{2,1,0:T(8,128)(2,1)}, u32[]{:S(2)}) copy-start(bf16[1,512,512]{2,1,0:T(8,128)(2,1)} %param.11) | copy-start | bytes 1572868
  142.5 4.6 %copy-start = (bf16[8,1,128,512]{2,3,1,0:T(8,128)(2,1)S(1)}, bf16[8,1,128,512]{2,3,1,0:T(8,128)(2,1)}, u32[]{:S(2)}) copy-start(bf16[8,1,128,512]{2,3,1,0:T(8,128)(2,1)} %get-tuple-element.7) | copy-start | bytes 3145732
  147.1 1.2 copy-start.3
  150.5 53.0 %all-to-all-start.3 = ((f32[8,128,512]{1,2,0:T(8,128)}), f32[8,128,512]{1,2,0:T(8,128)S(1)}, u32[]{:S(2)}, u32[]{:S(2)}) async-start(f32[8,128,512]{1,2,0:T(8,128)} %bitcast.62), calls=%async_computation.4 | async-start | bytes 4194304 | tf_op jit(solution)/shard_map/all_to_all | solution.py:38
Sparse Core Ops, SparseCore 0:
  78.7 63.7 all-gather.1
  145.3 73.9 reduce-scatter.1

commit v2 on v1

--- a/solution.py
+++ b/solution.py
@@ -8,6 +8,10 @@
 REP = ("z", "y_hi", "core")
 COLUMN = ("z", "y_hi")
 FSDP = ("x", "y_lo")
+
+
+def swap(value, axis, mask):
+    return lax.ppermute(value, axis, [(i, i ^ mask) for i in range(lax.axis_size(axis))])
 
 
 def outer_update(local_weight, global_weight, outer_momentum):
@@ -24,7 +28,7 @@
     mine = lax.all_to_all(
         jnp.broadcast_to(updated, (columns, rows, width)), COLUMN, 0, 0, tiled=True
     )
-    other = lax.ppermute(mine, "core", [(0, 1), (1, 0)])
+    other = swap(mine, "core", 1)
     first = lax.axis_index("core") == 0
     landed = jnp.stack(
         [jnp.where(first, mine, other), jnp.where(first, other, mine)], axis=1
@@ -32,13 +36,32 @@
     return (updated, momentum, landed)
 
 
-def keys_by_exchange(product):
-    parts = lax.axis_size(FSDP)
+def features_by_slot(hidden):
+    wide, near = lax.axis_size("x"), lax.axis_size("y_lo")
+    width = hidden.shape[2] // (wide * near)
+    slots = []
+    for a in range(wide):
+        for b in range(near):
+            block = (lax.axis_index("x") ^ a) * near + (lax.axis_index("y_lo") ^ b)
+            piece = lax.dynamic_slice_in_dim(hidden, block * width, width, 2)
+            slots.append(lax.ppermute(piece, FSDP, [(i, i ^ (a * near + b)) for i in range(wide * near)]) if a + b else piece)
+    return slots
+
+
+def cotangents_by_slot(cotangent):
+    pair = jnp.stack([cotangent, swap(cotangent, "y_lo", 1)], axis=1)
+    slots = [pair] + [swap(pair, "x", a) for a in range(1, lax.axis_size("x"))]
+    return jnp.concatenate(slots, axis=1)
+
+
+def keys_from_slots(product):
+    wide, near = lax.axis_size("x"), lax.axis_size("y_lo")
     rows, width = product.shape
-    pieces = lax.all_to_all(
-        product.reshape(parts, rows // parts, width), FSDP, 0, 0, tiled=True
-    )
-    return jnp.sum(pieces, axis=0)
+    slots = product.reshape(wide, near, rows // (wide * near), width)
+    total = slots[0]
+    for a in range(1, wide):
+        total = total + swap(slots[a], "x", a)
+    return total[0] + swap(total[1], "y_lo", 1)
 
 
 def per_device(
@@ -52,13 +75,9 @@
     step_count,
 ):
     factor = D ** (-0.5)
-    parts = lax.axis_size(FSDP)
-    tokens = hidden.shape[1]
-    width = hidden.shape[2] // parts
-    cotangents = lax.all_gather(cotangent, FSDP, axis=1, tiled=True)
+    pieces = features_by_slot(hidden)
+    cotangents = cotangents_by_slot(cotangent)
     updated, momentum, landed = outer_update(local_weight, global_weight, outer_momentum)
-    by_owner = hidden.reshape(STEPS, tokens, parts, width).transpose(2, 0, 1, 3)
-    columns = lax.all_to_all(by_owner, FSDP, 0, 0, tiled=True)
     weight = local_weight[0].astype(jnp.float32)
     moment_one = first_moment[0].astype(jnp.float32)
     moment_two = second_moment[0].astype(jnp.float32)
@@ -66,15 +85,12 @@
     key_list = []
     for inner in range(STEPS):
         weight_bf = weight.astype(jnp.bfloat16)
-        step_columns = columns[:, inner].reshape(parts * tokens, width)
-        step_upstream = cotangents[inner]
+        step_columns = jnp.concatenate([piece[inner] for piece in pieces], axis=0)
+        step_upstream = cotangents[inner].reshape(step_columns.shape[0], -1)
         product = lax.dot_general(
             step_columns, weight_bf, (((1,), (1,)), ((), ())), preferred_element_type=jnp.float32
         )
-        if inner == 0:
-            key_rows = lax.psum_scatter(product, FSDP, scatter_dimension=0, tiled=True)
-        else:
-            key_rows = keys_by_exchange(product)
+        key_rows = keys_from_slots(product)
         key_list.append((key_rows * factor).astype(jnp.bfloat16))
         gradient = (
             lax.dot_general(

time: 229 us -> 154 us (0.67)
  waiting for transfers between devices: 131 us -> 21.4 us
  starting transfers between devices: 16 us -> 97.9 us
  blocking collectives: 38.4 us -> 0 us
  between operations: 15 us -> 1.96 us
  local copies, waits for them, and re-layouts: 10.5 us -> 18.9 us
  matrix products: 12.1 us -> 7.84 us
    all_to_all x2 -> x1, waiting for transfers between devices: 69.8 us -> 0.01 us  [outer_update(): lax.all_to_all(local_weight[0].reshape(replicas, rows, width), REP, 0, 0,...]
    ppermute x1 -> x20, starting transfers between devices: 3.84 us -> 68.8 us  [the longest x13 45.4 us: swap(): lax.ppermute(value, axis, [(i, i ^ mask) for i in range(lax.axis_size(axi...]
    all_to_all x1 -> x0, blocking collectives: 38.4 us -> none  [outer_update(): lax.all_to_all(local_weight[0].reshape(replicas, rows, width), REP, 0, 0,...]
    all_gather x1 -> x0, waiting for transfers between devices: 29.9 us -> none  [per_device(): cotangents = lax.all_gather(cotangent, FSDP, axis=1, tiled=True)]
    ppermute x1 -> x20, waiting for transfers between devices: 0.78 us -> 21.4 us  [the longest x13 21.1 us: swap(): lax.ppermute(value, axis, [(i, i ^ mask) for i in range(lax.axis_size(axi...]
    reduce_scatter x1 -> x0, waiting for transfers between devices: 15.5 us -> none  [per_device(): key_rows = lax.psum_scatter(product, FSDP, scatter_dimension=0, tiled=True)]
    all_to_all x1, waiting for transfers between devices: 14.8 us -> 0.01 us  [outer_update(): lax.all_to_all(jnp.broadcast_to(updated, (columns, rows, width)), COLUMN,...]
    all_to_all x2 -> x1, starting transfers between devices: 7.63 us -> 17.3 us  [outer_update(): lax.all_to_all(local_weight[0].reshape(replicas, rows, width), REP, 0, 0,...]
  transfers between devices with their start and end apart: 6 -> 22, of which waited for: 6 -> 5; matrix products, arithmetic and copies ran while one was open for 10% -> 18% of each run, Pallas kernels for 0% -> 0%
where the time goes in v2:
time: 154 us; the launch traced here: 152 us
  starting transfers between devices  97.9 us (64%)
  waiting for transfers between devices  21.4 us (14%)
  local copies, waits for them, and re-layouts  18.9 us (12%)
  matrix products  7.84 us (5%)
  other arithmetic  4.33 us (3%)
  between operations  1.96 us (1%)
    ppermute x13, starting transfers between devices, swap(): lax.ppermute(value, axis, [(i, i ^ mask) for i in range(lax.axis_size(axi...  45.4 us
    ppermute x7, starting transfers between devices, features_by_slot(): lax.ppermute(piece, FSDP, [(i, i ^ a * near + b) for i in range(wide * ne...  23.3 us
    ppermute x13, waiting for transfers between devices, swap(): lax.ppermute(value, axis, [(i, i ^ mask) for i in range(lax.axis_size(axi...  21.1 us
    all_to_all x1, starting transfers between devices, outer_update(): lax.all_to_all(local_weight[0].reshape(replicas, rows, width), REP, 0, 0,...  17.3 us
    unnamed x27, local copies, waits for them, and re-layouts  11.9 us
    all_to_all x1, starting transfers between devices, outer_update(): lax.all_to_all(jnp.broadcast_to(updated, (columns, rows, width)), COLUMN,...  11.8 us
    dot_general x2, matrix products, per_device(): lax.dot_general(step_upstream, step_columns, (((0,), (0,)), ((), ())), pr...  5 us
  transfers between devices with their start and end apart: 22, of which 5 were waited for; matrix products, arithmetic and copies ran while one was open for 18% of the time, Pallas kernels for 0%

profile of v2, /device:TPU:1, one launch (start us, length us, event | category | flops | bytes accessed | tf_op | source)
XLA Modules:
  0.0 152.4 jit_solution(2881108930432300629)
XLA Ops:
  0.7 2.7 %constant_dynamic-slice_fusion = (bf16[2,128,512]{2,1,0:T(8,128)(2,1)}, bf16[2,128,512]{2,1,0:T(8,128)(2,1)}, bf16[2,128,512]{2,1,0:T(8,128)(2,1)}, bf16[2,128,5...) fusion(bf16[2,128,4096]{2,1,0:T(8,128)(2,1)} %param.8, ...), kind=kLoop, calls=%fused_computation.74 | loop fusion | bytes 3670044 | tf_op jit(solution)/shard_map/dynamic_slice | solution.py:46
  3.4 4.0 %collective-permute-start = (bf16[2,128,512]{2,1,0:T(8,128)(2,1)}, bf16[2,128,512]{2,1,0:T(8,128)(2,1)}, u32[]{:S(2)}, u32[]{:S(2)}) collective-permute-start(bf16[2,128,512]{2,1,0:T(8,128)(2,1)} %get-tuple-element.25), channel_id=1, source_target_pairs={{0,1},{1,0},{2,3},{3,2},{4,5},{5,4},{6,7},{7,6},{8,9},{9,8},{10,11... | collective-permute-start | bytes 786440 | tf_op jit(solution)/shard_map/ppermute | solution.py:47
  7.4 3.1 %collective-permute-start.1 = (bf16[2,128,512]{2,1,0:T(8,128)(2,1)}, bf16[2,128,512]{2,1,0:T(8,128)(2,1)}, u32[]{:S(2)}, u32[]{:S(2)}) collective-permute-start(bf16[2,128,512]{2,1,0:T(8,128)(2,1)} %get-tuple-element.24), channel_id=1, source_target_pairs={{0,2},{1,3},{2,0},{3,1},{4,6},{5,7},{6,4},{7,5},{8,10},{9,11},{10,... | collective-permute-start | bytes 786440 | tf_op jit(solution)/shard_map/ppermute | solution.py:47
  10.5 1.9 %collective-permute-start.2 = (bf16[2,128,512]{2,1,0:T(8,128)(2,1)}, bf16[2,128,512]{2,1,0:T(8,128)(2,1)}, u32[]{:S(2)}, u32[]{:S(2)}) collective-permute-start(bf16[2,128,512]{2,1,0:T(8,128)(2,1)} %get-tuple-element.23), channel_id=1, source_target_pairs={{0,3},{1,2},{2,1},{3,0},{4,7},{5,6},{6,5},{7,4},{8,11},{9,10},{10,... | collective-permute-start | bytes 786440 | tf_op jit(solution)/shard_map/ppermute | solution.py:47
  12.5 4.8 %collective-permute-start.3 = (bf16[2,128,512]{2,1,0:T(8,128)(2,1)}, bf16[2,128,512]{2,1,0:T(8,128)(2,1)S(1)}, u32[]{:S(2)}, u32[]{:S(2)}) collective-permute-start(bf16[2,128,512]{2,1,0:T(8,128)(2,1)} %get-tuple-element.22), channel_id=1, source_target_pairs={{0,4},{1,5},{2,6},{3,7},{4,0},{5,1},{6,2},{7,3},{8,12},{9,13},{10,... | collective-permute-start | bytes 786440 | tf_op jit(solution)/shard_map/ppermute | solution.py:47
  17.3 3.2 %collective-permute-start.11 = (bf16[2,128,512]{2,1,0:T(8,128)(2,1)S(1)}, bf16[2,128,512]{2,1,0:T(8,128)(2,1)S(1)}, u32[]{:S(2)}, u32[]{:S(2)}) collective-permute-start(bf16[2,128,512]{2,1,0:T(8,128)(2,1)S(1)} %copy-done.2), channel_id=1, source_target_pairs={{0,1},{1,0},{2,3},{3,2},{4,5},{5,4},{6,7},{7,6},{8,9},{9,8},{10,11... | collective-permute-start | bytes 786440 | tf_op jit(solution)/shard_map/ppermute | solution.py:14
  20.5 17.3 %all-to-all-start = ((bf16[64,8,512]{2,1,0:T(8,128)(2,1)}), bf16[64,8,512]{2,1,0:T(8,128)(2,1)S(1)}, u32[]{:S(2)}, u32[]{:S(2)}) async-start(bf16[64,8,512]{2,1,0:T(8,128)(2,1)} %bitcast.31), calls=%async_computation | async-start | bytes 1048576 | tf_op jit(solution)/shard_map/all_to_all | solution.py:20
  37.8 1.7 %fusion.31 = (bf16[1024,512]{1,0:T(8,128)(2,1)}, bf16[1024,512]{1,0:T(8,128)(2,1)}) fusion(bf16[2,128,4096]{2,1,0:T(8,128)(2,1)} %param.8, s32[]{:T(128)S(6)} %select_n.36, s32[]{:T(128)S(6)} %add.151), kind=kLoop, calls=%fused_computation.65 | loop fusion | bytes 524296
  40.4 0.0 collective-permute-done
  40.4 2.9 %collective-permute-start.4 = (bf16[2,128,512]{2,1,0:T(8,128)(2,1)}, bf16[2,128,512]{2,1,0:T(8,128)(2,1)S(1)}, u32[]{:S(2)}, u32[]{:S(2)}) collective-permute-start(bf16[2,128,512]{2,1,0:T(8,128)(2,1)} %get-tuple-element.21), channel_id=1, source_target_pairs={{0,5},{1,4},{2,7},{3,6},{4,1},{5,0},{6,3},{7,2},{8,13},{9,12},{10,... | collective-permute-start | bytes 786440 | tf_op jit(solution)/shard_map/ppermute | solution.py:47
  43.3 1.7 %fusion.30 = (bf16[1024,512]{1,0:T(8,128)(2,1)}, bf16[1024,512]{1,0:T(8,128)(2,1)}) fusion(bf16[1024,512]{1,0:T(8,128)(2,1)} %get-tuple-element.16, bf16[2,128,512]{2,1,0:T(8,128)(2,1)} %collective-permute-done, bf16[1024,512]{1,0:T(8,128)(2,1)} %get-tuple-element.17), kind=kLoop, calls=%fused_computation.63 | loop fusion | bytes 524288
  45.0 0.0 collective-permute-done.1
  45.0 4.4 %collective-permute-start.5 = (bf16[2,128,512]{2,1,0:T(8,128)(2,1)}, bf16[2,128,512]{2,1,0:T(8,128)(2,1)S(1)}, u32[]{:S(2)}, u32[]{:S(2)}) collective-permute-start(bf16[2,128,512]{2,1,0:T(8,128)(2,1)} %get-tuple-element.26), channel_id=1, source_target_pairs={{0,6},{1,7},{2,4},{3,5},{4,2},{5,3},{6,0},{7,1},{8,14},{9,15},{10,... | collective-permute-start | bytes 786440 | tf_op jit(solution)/shard_map/ppermute | solution.py:47
  49.4 1.7 %fusion.29 = (bf16[1024,512]{1,0:T(8,128)(2,1)}, bf16[1024,512]{1,0:T(8,128)(2,1)}) fusion(bf16[1024,512]{1,0:T(8,128)(2,1)} %get-tuple-element.41, bf16[2,128,512]{2,1,0:T(8,128)(2,1)} %collective-permute-done.1, bf16[1024,512]{1,0:T(8,128)(2,1)} %get-tuple-element.42), kind=kLoop, calls=%fused_computation.61 | loop fusion | bytes 524288
  51.1 2.2 %collective-permute-start.6 = (bf16[2,128,512]{2,1,0:T(8,128)(2,1)}, bf16[2,128,512]{2,1,0:T(8,128)(2,1)S(1)}, u32[]{:S(2)}, u32[]{:S(2)}) collective-permute-start(bf16[2,128,512]{2,1,0:T(8,128)(2,1)} %get-tuple-element.20), channel_id=1, source_target_pairs={{0,7},{1,6},{2,5},{3,4},{4,3},{5,2},{6,1},{7,0},{8,15},{9,14},{10,... | collective-permute-start | bytes 786440 | tf_op jit(solution)/shard_map/ppermute | solution.py:47
  53.3 0.0 copy-start.4
  53.3 0.0 copy-start.5
  53.3 0.8 pad_maximum_fusion.1
  54.2 1.9 %collective-permute-start.12 = (bf16[2,2,128,512]{3,2,0,1:T(8,128)(2,1)}, bf16[2,2,128,512]{3,2,0,1:T(8,128)(2,1)}, u32[]{:S(2)}, u32[]{:S(2)}) collective-permute-start(bf16[2,2,128,512]{3,2,0,1:T(8,128)(2,1)} %pad_maximum_fusion.1), channel_id=1, source_target_pairs={{0,2},{2,0},{4,6},{6,4},{1,3},{3,1},{5,7},{7,5},{8,10},{10,8},{12,... | collective-permute-start | bytes 1572872 | tf_op jit(solution)/shard_map/ppermute | solution.py:14
  56.1 1.7 %fusion.28 = (bf16[1024,512]{1,0:T(8,128)(2,1)}, bf16[1024,512]{1,0:T(8,128)(2,1)}) fusion(bf16[1024,512]{1,0:T(8,128)(2,1)} %get-tuple-element.39, bf16[2,128,512]{2,1,0:T(8,128)(2,1)} %collective-permute-done.2, bf16[1024,512]{1,0:T(8,128)(2,1)} %get-tuple-element.40), kind=kLoop, calls=%fused_computation.59 | loop fusion | bytes 524288
  57.8 5.5 %collective-permute-start.13 = (bf16[2,2,128,512]{3,2,0,1:T(8,128)(2,1)}, bf16[2,2,128,512]{3,2,0,1:T(8,128)(2,1)}, u32[]{:S(2)}, u32[]{:S(2)}) collective-permute-start(bf16[2,2,128,512]{3,2,0,1:T(8,128)(2,1)} %pad_maximum_fusion.1), channel_id=1, source_target_pairs={{0,4},{2,6},{4,0},{6,2},{1,5},{3,7},{5,1},{7,3},{8,12},{10,14},{12... | collective-permute-start | bytes 1572872 | tf_op jit(solution)/shard_map/ppermute | solution.py:14
  63.3 0.7 fusion.27
  64.1 2.1 %collective-permute-start.14 = (bf16[2,2,128,512]{3,2,0,1:T(8,128)(2,1)}, bf16[2,2,128,512]{3,2,0,1:T(8,128)(2,1)}, u32[]{:S(2)}, u32[]{:S(2)}) collective-permute-start(bf16[2,2,128,512]{3,2,0,1:T(8,128)(2,1)} %pad_maximum_fusion.1), channel_id=1, source_target_pairs={{0,6},{2,4},{4,2},{6,0},{1,7},{3,5},{5,3},{7,1},{8,14},{10,12},{12... | collective-permute-start | bytes 1572872 | tf_op jit(solution)/shard_map/ppermute | solution.py:14
  66.2 0.7 fusion.26
  66.9 0.3 collective-permute-done.5
  67.2 0.7 fusion.25
  67.9 0.7 fusion.24
  68.6 0.1 convert_reduce_fusion
  68.8 0.6 multiply_subtract_fusion
  69.4 0.9 broadcast_in_dim.6
  70.2 11.8 %all-to-all-start.1 = ((f32[32,8,512]{2,1,0:T(8,128)}), f32[32,8,512]{2,1,0:T(8,128)S(1)}, u32[]{:S(2)}, u32[]{:S(2)}) async-start(f32[32,8,512]{2,1,0:T(8,128)} %broadcast_in_dim.6), calls=%async_computation.1 | async-start | bytes 1048576 | tf_op jit(solution)/shard_map/all_to_all | solution.py:28
  82.1 2.1 %fusion.4 = f32[1024,512]{1,0:T(8,128)S(1)} fusion(bf16[1024,512]{1,0:T(8,128)(2,1)} %get-tuple-element.29, bf16[1,512,512]{2,1,0:T(8,128)(2,1)} %param.10), kind=kOutput, calls=%fused_computation.13 | convolution fusion | flops 536870912 | bytes 3670016 | tf_op jit(solution)/shard_map/dot_general | solution.py:90
  84.2 1.2 fusion.34
  85.4 4.4 %collective-permute-start.9 = (f32[2,128,512]{2,1,0:T(8,128)}, f32[2,128,512]{2,1,0:T(8,128)}, u32[]{:S(2)}, u32[]{:S(2)}) collective-permute-start(f32[2,128,512]{2,1,0:T(8,128)} %bitcast.12), channel_id=1, source_target_pairs={{0,6},{2,4},{4,2},{6,0},{1,7},{3,5},{5,3},{7,1},{8,14},{10,12},{12... | collective-permute-start | bytes 1572872 | tf_op jit(solution)/shard_map/ppermute | solution.py:14
  89.7 1.9 %collective-permute-start.8 = (f32[2,128,512]{2,1,0:T(8,128)}, f32[2,128,512]{2,1,0:T(8,128)}, u32[]{:S(2)}, u32[]{:S(2)}) collective-permute-start(f32[2,128,512]{2,1,0:T(8,128)} %bitcast.11), channel_id=1, source_target_pairs={{0,4},{2,6},{4,0},{6,2},{1,5},{3,7},{5,1},{7,3},{8,12},{10,14},{12... | collective-permute-start | bytes 1572872 | tf_op jit(solution)/shard_map/ppermute | solution.py:14
  91.7 2.7 %collective-permute-start.7 = (f32[2,128,512]{2,1,0:T(8,128)}, f32[2,128,512]{2,1,0:T(8,128)}, u32[]{:S(2)}, u32[]{:S(2)}) collective-permute-start(f32[2,128,512]{2,1,0:T(8,128)} %bitcast.10), channel_id=1, source_target_pairs={{0,2},{2,0},{4,6},{6,4},{1,3},{3,1},{5,7},{7,5},{8,10},{10,8},{12,... | collective-permute-start | bytes 1572872 | tf_op jit(solution)/shard_map/ppermute | solution.py:14
  94.4 1.1 constant_dynamic-update-slice_fusion.2
  95.5 1.1 constant_dynamic-update-slice_fusion.1
  96.6 1.1 constant_dynamic-update-slice_fusion
  97.7 5.1 %collective-permute-start.15 = (f32[32,8,512]{2,1,0:T(8,128)S(1)}, f32[32,8,512]{2,1,0:T(8,128)S(1)}, u32[]{:S(2)}, u32[]{:S(2)}) collective-permute-start(f32[32,8,512]{2,1,0:T(8,128)S(1)} %all-to-all-done.1), channel_id=1, source_target_pairs={{0,8},{8,0},{1,9},{9,1},{2,10},{10,2},{3,11},{11,3},{4,12},{12,4},... | collective-permute-start | bytes 1572872 | tf_op jit(solution)/shard_map/ppermute | solution.py:14
  102.8 0.2 fusion.36
  103.0 0.7 fusion.37
  103.8 0.0 copy-start.6
  103.8 0.0 copy-start.7
  103.8 0.5 collective-permute-done.15
  104.3 0.1 select_bitcast_fusion.1
  104.4 0.1 pad_maximum_fusion
  104.5 0.5 copy-done.1
  105.0 0.1 copy-done.6
  105.1 0.2 copy-done.7
  105.3 4.3 %fusion.7 = (bf16[1,512,512]{2,1,0:T(8,128)(2,1)}, f32[512,512]{1,0:T(8,128)S(1)}) fusion(f32[]{:T(128)} %bitcast.45, f32[512,512]{1,0:T(8,128)S(1)} %fusion.37, bf16[1,512,512]{2,1,0:T(8,128)(2,1)S(1)} %copy-done.6, f32[]{:T(128)} %bitcast.44, bf16[1,512,512]{2,1,0:T(8,128)(2,1)S(1)} %copy-done.7, f32[32,2,8,512]{3,2,1,0:T(8,128)S(1)} %pad_maximum_fusion, ...), kind=kOutput, calls=%fused_computation.20 | convolution fusion | flops 546832384 | bytes 7340048 | tf_op jit(solution)/shard_map/dot_general | solution.py:96
  109.6 0.7 fusion.3
  110.3 0.2 fusion.35
  110.5 4.4 %collective-permute-start.18 = (f32[2,128,512]{2,1,0:T(8,128)S(1)}, f32[2,128,512]{2,1,0:T(8,128)S(1)}, u32[]{:S(2)}, u32[]{:S(2)}) collective-permute-start(f32[2,128,512]{2,1,0:T(8,128)S(1)} %bitcast.159), channel_id=1, source_target_pairs={{0,6},{2,4},{4,2},{6,0},{1,7},{3,5},{5,3},{7,1},{8,14},{10,12},{12... | collective-permute-start | bytes 1572872 | tf_op jit(solution)/shard_map/ppermute | solution.py:14
  114.9 3.8 %collective-permute-start.17 = (f32[2,128,512]{2,1,0:T(8,128)S(1)}, f32[2,128,512]{2,1,0:T(8,128)S(1)}, u32[]{:S(2)}, u32[]{:S(2)}) collective-permute-start(f32[2,128,512]{2,1,0:T(8,128)S(1)} %bitcast.158), channel_id=1, source_target_pairs={{0,4},{2,6},{4,0},{6,2},{1,5},{3,7},{5,1},{7,3},{8,12},{10,14},{12... | collective-permute-start | bytes 1572872 | tf_op jit(solution)/shard_map/ppermute | solution.py:14
  118.7 1.9 %collective-permute-start.16 = (f32[2,128,512]{2,1,0:T(8,128)S(1)}, f32[2,128,512]{2,1,0:T(8,128)S(1)}, u32[]{:S(2)}, u32[]{:S(2)}) collective-permute-start(f32[2,128,512]{2,1,0:T(8,128)S(1)} %bitcast.157), channel_id=1, source_target_pairs={{0,2},{2,0},{4,6},{6,4},{1,3},{3,1},{5,7},{7,5},{8,10},{10,8},{12,... | collective-permute-start | bytes 1572872 | tf_op jit(solution)/shard_map/ppermute | solution.py:14
  120.6 1.6 %add_add_fusion.1 = f32[2,128,512]{2,1,0:T(8,128)S(1)} fusion(f32[2,128,512]{2,1,0:T(8,128)} %collective-permute-done.9, f32[2,128,512]{2,1,0:T(8,128)} %collective-permute-done.8, f32[2,128,512]{2,1,0:T(8,128)S(1)} %bitcast.151, f32[2,128,512]{2,1,0:T(8,128)} %collective-permute-done.7), kind=kLoop, calls=%fused_computation.19 | loop fusion | flops 393216 | bytes 2621440 | tf_op jit(solution)/shard_map/add | solution.py:63
  122.2 4.1 %collective-permute-start.10 = (f32[128,512]{1,0:T(8,128)S(1)}, f32[128,512]{1,0:T(8,128)S(1)}, u32[]{:S(2)}, u32[]{:S(2)}) collective-permute-start(f32[128,512]{1,0:T(8,128)S(1)} %slice_bitcast_fusion.2), channel_id=1, source_target_pairs={{0,1},{1,0},{2,3},{3,2},{4,5},{5,4},{6,7},{7,6},{8,9},{9,8},{10,11... | collective-permute-start | bytes 786440 | tf_op jit(solution)/shard_map/ppermute | solution.py:14
  126.3 12.0 %collective-permute-done.18 = f32[2,128,512]{2,1,0:T(8,128)S(1)} collective-permute-done((f32[2,128,512]{2,1,0:T(8,128)S(1)}, f32[2,128,512]{2,1,0:T(8,128)S(1)}, u32[]{:S(2)}, u32[]{:S(2)}) %collective-permute-start.18) | collective-permute-done | bytes 524320 | tf_op jit(solution)/shard_map/ppermute | solution.py:14
  138.4 3.1 %collective-permute-done.16 = f32[2,128,512]{2,1,0:T(8,128)S(1)} collective-permute-done((f32[2,128,512]{2,1,0:T(8,128)S(1)}, f32[2,128,512]{2,1,0:T(8,128)S(1)}, u32[]{:S(2)}, u32[]{:S(2)}) %collective-permute-start.16) | collective-permute-done | bytes 524320 | tf_op jit(solution)/shard_map/ppermute | solution.py:14
  141.4 0.2 add_add_fusion
  141.7 4.4 %collective-permute-start.19 = (f32[128,512]{1,0:T(8,128)S(1)}, f32[128,512]{1,0:T(8,128)S(1)}, u32[]{:S(2)}, u32[]{:S(2)}) collective-permute-start(f32[128,512]{1,0:T(8,128)S(1)} %slice_bitcast_fusion), channel_id=1, source_target_pairs={{0,1},{1,0},{2,3},{3,2},{4,5},{5,4},{6,7},{7,6},{8,9},{9,8},{10,11... | collective-permute-start | bytes 786440 | tf_op jit(solution)/shard_map/ppermute | solution.py:14
  146.1 5.5 %collective-permute-done.19 = f32[128,512]{1,0:T(8,128)S(1)} collective-permute-done((f32[128,512]{1,0:T(8,128)S(1)}, f32[128,512]{1,0:T(8,128)S(1)}, u32[]{:S(2)}, u32[]{:S(2)}) %collective-permute-start.19) | collective-permute-done | bytes 262176 | tf_op jit(solution)/shard_map/ppermute | solution.py:14
  151.6 0.7 pad_maximum_fusion.2
  (30 shorter events, 0.2 us)
Async XLA Ops:
  0.6 16.6 %copy-start.2 = (bf16[2,128,512]{2,1,0:T(8,128)(2,1)S(1)}, bf16[2,128,512]{2,1,0:T(8,128)(2,1)}, u32[]{:S(2)}) copy-start(bf16[2,128,512]{2,1,0:T(8,128)(2,1)} %param.9) | copy-start | bytes 786436
  3.4 37.0 %collective-permute-start = (bf16[2,128,512]{2,1,0:T(8,128)(2,1)}, bf16[2,128,512]{2,1,0:T(8,128)(2,1)}, u32[]{:S(2)}, u32[]{:S(2)}) collective-permute-start(bf16[2,128,512]{2,1,0:T(8,128)(2,1)} %get-tuple-element.25), channel_id=1, source_target_pairs={{0,1},{1,0},{2,3},{3,2},{4,5},{5,4},{6,7},{7,6},{8,9},{9,8},{10,11... | collective-permute-start | bytes 786440 | tf_op jit(solution)/shard_map/ppermute | solution.py:47
  7.4 37.6 %collective-permute-start.1 = (bf16[2,128,512]{2,1,0:T(8,128)(2,1)}, bf16[2,128,512]{2,1,0:T(8,128)(2,1)}, u32[]{:S(2)}, u32[]{:S(2)}) collective-permute-start(bf16[2,128,512]{2,1,0:T(8,128)(2,1)} %get-tuple-element.24), channel_id=1, source_target_pairs={{0,2},{1,3},{2,0},{3,1},{4,6},{5,7},{6,4},{7,5},{8,10},{9,11},{10,... | collective-permute-start | bytes 786440 | tf_op jit(solution)/shard_map/ppermute | solution.py:47
  10.5 43.6 %collective-permute-start.2 = (bf16[2,128,512]{2,1,0:T(8,128)(2,1)}, bf16[2,128,512]{2,1,0:T(8,128)(2,1)}, u32[]{:S(2)}, u32[]{:S(2)}) collective-permute-start(bf16[2,128,512]{2,1,0:T(8,128)(2,1)} %get-tuple-element.23), channel_id=1, source_target_pairs={{0,3},{1,2},{2,1},{3,0},{4,7},{5,6},{6,5},{7,4},{8,11},{9,10},{10,... | collective-permute-start | bytes 786440 | tf_op jit(solution)/shard_map/ppermute | solution.py:47
  12.5 45.3 %collective-permute-start.3 = (bf16[2,128,512]{2,1,0:T(8,128)(2,1)}, bf16[2,128,512]{2,1,0:T(8,128)(2,1)S(1)}, u32[]{:S(2)}, u32[]{:S(2)}) collective-permute-start(bf16[2,128,512]{2,1,0:T(8,128)(2,1)} %get-tuple-element.22), channel_id=1, source_target_pairs={{0,4},{1,5},{2,6},{3,7},{4,0},{5,1},{6,2},{7,3},{8,12},{9,13},{10,... | collective-permute-start | bytes 786440 | tf_op jit(solution)/shard_map/ppermute | solution.py:47
  17.3 33.8 %collective-permute-start.11 = (bf16[2,128,512]{2,1,0:T(8,128)(2,1)S(1)}, bf16[2,128,512]{2,1,0:T(8,128)(2,1)S(1)}, u32[]{:S(2)}, u32[]{:S(2)}) collective-permute-start(bf16[2,128,512]{2,1,0:T(8,128)(2,1)S(1)} %copy-done.2), channel_id=1, source_target_pairs={{0,1},{1,0},{2,3},{3,2},{4,5},{5,4},{6,7},{7,6},{8,9},{9,8},{10,11... | collective-permute-start | bytes 786440 | tf_op jit(solution)/shard_map/ppermute | solution.py:14
  20.5 48.2 %all-to-all-start = ((bf16[64,8,512]{2,1,0:T(8,128)(2,1)}), bf16[64,8,512]{2,1,0:T(8,128)(2,1)S(1)}, u32[]{:S(2)}, u32[]{:S(2)}) async-start(bf16[64,8,512]{2,1,0:T(8,128)(2,1)} %bitcast.31), calls=%async_computation | async-start | bytes 1048576 | tf_op jit(solution)/shard_map/all_to_all | solution.py:20
  40.4 23.7 %collective-permute-start.4 = (bf16[2,128,512]{2,1,0:T(8,128)(2,1)}, bf16[2,128,512]{2,1,0:T(8,128)(2,1)S(1)}, u32[]{:S(2)}, u32[]{:S(2)}) collective-permute-start(bf16[2,128,512]{2,1,0:T(8,128)(2,1)} %get-tuple-element.21), channel_id=1, source_target_pairs={{0,5},{1,4},{2,7},{3,6},{4,1},{5,0},{6,3},{7,2},{8,13},{9,12},{10,... | collective-permute-start | bytes 786440 | tf_op jit(solution)/shard_map/ppermute | solution.py:47
  45.0 22.2 %collective-permute-start.5 = (bf16[2,128,512]{2,1,0:T(8,128)(2,1)}, bf16[2,128,512]{2,1,0:T(8,128)(2,1)S(1)}, u32[]{:S(2)}, u32[]{:S(2)}) collective-permute-start(bf16[2,128,512]{2,1,0:T(8,128)(2,1)} %get-tuple-element.26), channel_id=1, source_target_pairs={{0,6},{1,7},{2,4},{3,5},{4,2},{5,3},{6,0},{7,1},{8,14},{9,15},{10,... | collective-permute-start | bytes 786440 | tf_op jit(solution)/shard_map/ppermute | solution.py:47
  51.1 16.8 %collective-permute-start.6 = (bf16[2,128,512]{2,1,0:T(8,128)(2,1)}, bf16[2,128,512]{2,1,0:T(8,128)(2,1)S(1)}, u32[]{:S(2)}, u32[]{:S(2)}) collective-permute-start(bf16[2,128,512]{2,1,0:T(8,128)(2,1)} %get-tuple-element.20), channel_id=1, source_target_pairs={{0,7},{1,6},{2,5},{3,4},{4,3},{5,2},{6,1},{7,0},{8,15},{9,14},{10,... | collective-permute-start | bytes 786440 | tf_op jit(solution)/shard_map/ppermute | solution.py:47
  53.3 15.4 %copy-start.4 = (f32[8,512]{1,0:T(8,128)S(1)}, f32[8,512]{1,0:T(8,128)}, u32[]{:S(2)}) copy-start(f32[8,512]{1,0:T(8,128)} %param.13) | copy-start | bytes 49156
  53.3 15.4 %copy-start.5 = (f32[8,512]{1,0:T(8,128)S(1)}, f32[8,512]{1,0:T(8,128)}, u32[]{:S(2)}) copy-start(f32[8,512]{1,0:T(8,128)} %param.14) | copy-start | bytes 49156
  54.2 37.5 %collective-permute-start.12 = (bf16[2,2,128,512]{3,2,0,1:T(8,128)(2,1)}, bf16[2,2,128,512]{3,2,0,1:T(8,128)(2,1)}, u32[]{:S(2)}, u32[]{:S(2)}) collective-permute-start(bf16[2,2,128,512]{3,2,0,1:T(8,128)(2,1)} %pad_maximum_fusion.1), channel_id=1, source_target_pairs={{0,2},{2,0},{4,6},{6,4},{1,3},{3,1},{5,7},{7,5},{8,10},{10,8},{12,... | collective-permute-start | bytes 1572872 | tf_op jit(solution)/shard_map/ppermute | solution.py:14
  57.8 37.7 %collective-permute-start.13 = (bf16[2,2,128,512]{3,2,0,1:T(8,128)(2,1)}, bf16[2,2,128,512]{3,2,0,1:T(8,128)(2,1)}, u32[]{:S(2)}, u32[]{:S(2)}) collective-permute-start(bf16[2,2,128,512]{3,2,0,1:T(8,128)(2,1)} %pad_maximum_fusion.1), channel_id=1, source_target_pairs={{0,4},{2,6},{4,0},{6,2},{1,5},{3,7},{5,1},{7,3},{8,12},{10,14},{12... | collective-permute-start | bytes 1572872 | tf_op jit(solution)/shard_map/ppermute | solution.py:14
  64.1 32.5 %collective-permute-start.14 = (bf16[2,2,128,512]{3,2,0,1:T(8,128)(2,1)}, bf16[2,2,128,512]{3,2,0,1:T(8,128)(2,1)}, u32[]{:S(2)}, u32[]{:S(2)}) collective-permute-start(bf16[2,2,128,512]{3,2,0,1:T(8,128)(2,1)} %pad_maximum_fusion.1), channel_id=1, source_target_pairs={{0,6},{2,4},{4,2},{6,0},{1,7},{3,5},{5,3},{7,1},{8,14},{10,12},{12... | collective-permute-start | bytes 1572872 | tf_op jit(solution)/shard_map/ppermute | solution.py:14
  69.4 14.8 %copy-start.3 = (f32[8,512]{1,0:T(8,128)}, f32[8,512]{1,0:T(8,128)S(1)}, u32[]{:S(2)}) copy-start(f32[8,512]{1,0:T(8,128)S(1)} %get-tuple-element.6) | copy-start | bytes 49156
  70.2 27.4 %all-to-all-start.1 = ((f32[32,8,512]{2,1,0:T(8,128)}), f32[32,8,512]{2,1,0:T(8,128)S(1)}, u32[]{:S(2)}, u32[]{:S(2)}) async-start(f32[32,8,512]{2,1,0:T(8,128)} %broadcast_in_dim.6), calls=%async_computation.1 | async-start | bytes 1048576 | tf_op jit(solution)/shard_map/all_to_all | solution.py:28
  85.4 33.3 %collective-permute-start.9 = (f32[2,128,512]{2,1,0:T(8,128)}, f32[2,128,512]{2,1,0:T(8,128)}, u32[]{:S(2)}, u32[]{:S(2)}) collective-permute-start(f32[2,128,512]{2,1,0:T(8,128)} %bitcast.12), channel_id=1, source_target_pairs={{0,6},{2,4},{4,2},{6,0},{1,7},{3,5},{5,3},{7,1},{8,14},{10,12},{12... | collective-permute-start | bytes 1572872 | tf_op jit(solution)/shard_map/ppermute | solution.py:14
  89.7 30.9 %collective-permute-start.8 = (f32[2,128,512]{2,1,0:T(8,128)}, f32[2,128,512]{2,1,0:T(8,128)}, u32[]{:S(2)}, u32[]{:S(2)}) collective-permute-start(f32[2,128,512]{2,1,0:T(8,128)} %bitcast.11), channel_id=1, source_target_pairs={{0,4},{2,6},{4,0},{6,2},{1,5},{3,7},{5,1},{7,3},{8,12},{10,14},{12... | collective-permute-start | bytes 1572872 | tf_op jit(solution)/shard_map/ppermute | solution.py:14
  91.7 28.9 %collective-permute-start.7 = (f32[2,128,512]{2,1,0:T(8,128)}, f32[2,128,512]{2,1,0:T(8,128)}, u32[]{:S(2)}, u32[]{:S(2)}) collective-permute-start(f32[2,128,512]{2,1,0:T(8,128)} %bitcast.10), channel_id=1, source_target_pairs={{0,2},{2,0},{4,6},{6,4},{1,3},{3,1},{5,7},{7,5},{8,10},{10,8},{12,... | collective-permute-start | bytes 1572872 | tf_op jit(solution)/shard_map/ppermute | solution.py:14
  97.7 5.4 %copy-start = (bf16[1024,512]{1,0:T(8,128)(2,1)S(1)}, bf16[1024,512]{1,0:T(8,128)(2,1)}, u32[]{:S(2)}) copy-start(bf16[1024,512]{1,0:T(8,128)(2,1)} %get-tuple-element.29) | copy-start | bytes 3145732
  97.7 6.7 %collective-permute-start.15 = (f32[32,8,512]{2,1,0:T(8,128)S(1)}, f32[32,8,512]{2,1,0:T(8,128)S(1)}, u32[]{:S(2)}, u32[]{:S(2)}) collective-permute-start(f32[32,8,512]{2,1,0:T(8,128)S(1)} %all-to-all-done.1), channel_id=1, source_target_pairs={{0,8},{8,0},{1,9},{9,1},{2,10},{10,2},{3,11},{11,3},{4,12},{12,4},... | collective-permute-start | bytes 1572872 | tf_op jit(solution)/shard_map/ppermute | solution.py:14
  103.8 1.2 copy-start.1
  103.8 1.4 copy-start.6
  103.8 1.5 copy-start.7
  110.5 27.9 %collective-permute-start.18 = (f32[2,128,512]{2,1,0:T(8,128)S(1)}, f32[2,128,512]{2,1,0:T(8,128)S(1)}, u32[]{:S(2)}, u32[]{:S(2)}) collective-permute-start(f32[2,128,512]{2,1,0:T(8,128)S(1)} %bitcast.159), channel_id=1, source_target_pairs={{0,6},{2,4},{4,2},{6,0},{1,7},{3,5},{5,3},{7,1},{8,14},{10,12},{12... | collective-permute-start | bytes 1572872 | tf_op jit(solution)/shard_map/ppermute | solution.py:14
  114.9 23.5 %collective-permute-start.17 = (f32[2,128,512]{2,1,0:T(8,128)S(1)}, f32[2,128,512]{2,1,0:T(8,128)S(1)}, u32[]{:S(2)}, u32[]{:S(2)}) collective-permute-start(f32[2,128,512]{2,1,0:T(8,128)S(1)} %bitcast.158), channel_id=1, source_target_pairs={{0,4},{2,6},{4,0},{6,2},{1,5},{3,7},{5,1},{7,3},{8,12},{10,14},{12... | collective-permute-start | bytes 1572872 | tf_op jit(solution)/shard_map/ppermute | solution.py:14
  118.7 22.8 %collective-permute-start.16 = (f32[2,128,512]{2,1,0:T(8,128)S(1)}, f32[2,128,512]{2,1,0:T(8,128)S(1)}, u32[]{:S(2)}, u32[]{:S(2)}) collective-permute-start(f32[2,128,512]{2,1,0:T(8,128)S(1)} %bitcast.157), channel_id=1, source_target_pairs={{0,2},{2,0},{4,6},{6,4},{1,3},{3,1},{5,7},{7,5},{8,10},{10,8},{12,... | collective-permute-start | bytes 1572872 | tf_op jit(solution)/shard_map/ppermute | solution.py:14
  122.2 23.8 %collective-permute-start.10 = (f32[128,512]{1,0:T(8,128)S(1)}, f32[128,512]{1,0:T(8,128)S(1)}, u32[]{:S(2)}, u32[]{:S(2)}) collective-permute-start(f32[128,512]{1,0:T(8,128)S(1)} %slice_bitcast_fusion.2), channel_id=1, source_target_pairs={{0,1},{1,0},{2,3},{3,2},{4,5},{5,4},{6,7},{7,6},{8,9},{9,8},{10,11... | collective-permute-start | bytes 786440 | tf_op jit(solution)/shard_map/ppermute | solution.py:14
  141.7 9.9 %collective-permute-start.19 = (f32[128,512]{1,0:T(8,128)S(1)}, f32[128,512]{1,0:T(8,128)S(1)}, u32[]{:S(2)}, u32[]{:S(2)}) collective-permute-start(f32[128,512]{1,0:T(8,128)S(1)} %slice_bitcast_fusion), channel_id=1, source_target_pairs={{0,1},{1,0},{2,3},{3,2},{4,5},{5,4},{6,7},{7,6},{8,9},{9,8},{10,11... | collective-permute-start | bytes 786440 | tf_op jit(solution)/shard_map/ppermute | solution.py:14

commit v3 on v2

--- a/solution.py
+++ b/solution.py
@@ -36,22 +36,22 @@
     return (updated, momentum, landed)
 
 
-def features_by_slot(hidden):
+def features_by_slot(hidden, cotangent):
     wide, near = lax.axis_size("x"), lax.axis_size("y_lo")
     width = hidden.shape[2] // (wide * near)
-    slots = []
-    for a in range(wide):
-        for b in range(near):
-            block = (lax.axis_index("x") ^ a) * near + (lax.axis_index("y_lo") ^ b)
-            piece = lax.dynamic_slice_in_dim(hidden, block * width, width, 2)
-            slots.append(lax.ppermute(piece, FSDP, [(i, i ^ (a * near + b)) for i in range(wide * near)]) if a + b else piece)
-    return slots
-
-
-def cotangents_by_slot(cotangent):
-    pair = jnp.stack([cotangent, swap(cotangent, "y_lo", 1)], axis=1)
-    slots = [pair] + [swap(pair, "x", a) for a in range(1, lax.axis_size("x"))]
-    return jnp.concatenate(slots, axis=1)
+    slots = jnp.zeros((wide * near,) + hidden.shape[:2] + (width,), hidden.dtype)
+    place = lax.axis_index(FSDP)
+    for k in range(wide * near):
+        piece = lax.dynamic_slice_in_dim(hidden, (place ^ k) * width, width, 2)
+        if k == 1:
+            piece = jnp.concatenate([piece, cotangent])
+        landed = swap(piece, FSDP, k) if k else piece
+        if k == 1:
+            landed, near_cotangent = landed[: hidden.shape[0]], landed[hidden.shape[0] :]
+        slots = slots.at[k].set(landed)
+    pair = jnp.stack([cotangent, near_cotangent], axis=1)
+    pairs = [pair] + [swap(pair, "x", a) for a in range(1, wide)]
+    return slots, jnp.concatenate(pairs, axis=1)
 
 
 def keys_from_slots(product):
@@ -75,8 +75,7 @@
     step_count,
 ):
     factor = D ** (-0.5)
-    pieces = features_by_slot(hidden)
-    cotangents = cotangents_by_slot(cotangent)
+    pieces, cotangents = features_by_slot(hidden, cotangent)
     updated, momentum, landed = outer_update(local_weight, global_weight, outer_momentum)
     weight = local_weight[0].astype(jnp.float32)
     moment_one = first_moment[0].astype(jnp.float32)
@@ -85,7 +84,7 @@
     key_list = []
     for inner in range(STEPS):
         weight_bf = weight.astype(jnp.bfloat16)
-        step_columns = jnp.concatenate([piece[inner] for piece in pieces], axis=0)
+        step_columns = pieces[:, inner].reshape(-1, pieces.shape[3])
         step_upstream = cotangents[inner].reshape(step_columns.shape[0], -1)
         product = lax.dot_general(
             step_columns, weight_bf, (((1,), (1,)), ((), ())), preferred_element_type=jnp.float32

time: 154 us -> 149 us (0.968)
  starting transfers between devices: 97.9 us -> 90.4 us
  waiting for transfers between devices: 21.4 us -> 23.4 us
    ppermute x7 -> x0, starting transfers between devices: 23.3 us -> none  [features_by_slot(): lax.ppermute(piece, FSDP, [(i, i ^ a * near + b) for i in range(wide * ne...]
    ppermute x13 -> x19, starting transfers between devices: 45.4 us -> 61.2 us  [swap(): lax.ppermute(value, axis, [(i, i ^ mask) for i in range(lax.axis_size(axi...]
    unnamed x27 -> x20, local copies, waits for them, and re-layouts: 11.9 us -> 6.59 us
    scatter x0 -> x8, local copies, waits for them, and re-layouts: none -> 4.12 us  [features_by_slot(): slots = slots.at[k].set(landed)]
    ppermute x13 -> x19, waiting for transfers between devices: 21.1 us -> 23.4 us  [swap(): lax.ppermute(value, axis, [(i, i ^ mask) for i in range(lax.axis_size(axi...]
    slice x1, local copies, waits for them, and re-layouts: 0.2 us -> 1.75 us  [per_device(): step_upstream = cotangents[inner].reshape(step_columns.shape[0], -1)]
  transfers between devices with their start and end apart: 22 -> 21, of which waited for: 5 -> 3; matrix products, arithmetic and copies ran while one was open for 18% -> 18% of each run, Pallas kernels for 0% -> 0%
where the time goes in v3:
time: 149 us; the launch traced here: 147 us
  starting transfers between devices  90.4 us (61%)
  waiting for transfers between devices  23.4 us (16%)
  local copies, waits for them, and re-layouts  19.3 us (13%)
  matrix products  7.51 us (5%)
  other arithmetic  4.4 us (3%)
  between operations  1.98 us (1%)
    ppermute x19, starting transfers between devices, swap(): lax.ppermute(value, axis, [(i, i ^ mask) for i in range(lax.axis_size(axi...  61.2 us
    ppermute x19, waiting for transfers between devices, swap(): lax.ppermute(value, axis, [(i, i ^ mask) for i in range(lax.axis_size(axi...  23.4 us
    all_to_all x1, starting transfers between devices, outer_update(): lax.all_to_all(local_weight[0].reshape(replicas, rows, width), REP, 0, 0,...  17.3 us
    all_to_all x1, starting transfers between devices, outer_update(): lax.all_to_all(jnp.broadcast_to(updated, (columns, rows, width)), COLUMN,...  11.9 us
    unnamed x20, local copies, waits for them, and re-layouts  6.59 us
    dot_general x2, matrix products, per_device(): lax.dot_general(step_upstream, step_columns, (((0,), (0,)), ((), ())), pr...  4.99 us
    scatter x8, local copies, waits for them, and re-layouts, features_by_slot(): slots = slots.at[k].set(landed)  4.12 us
  transfers between devices with their start and end apart: 21, of which 3 were waited for; matrix products, arithmetic and copies ran while one was open for 18% of the time, Pallas kernels for 0%

profile of v3, /device:TPU:1, one launch (start us, length us, event | category | flops | bytes accessed | tf_op | source)
XLA Modules:
  0.0 146.9 jit_solution(8821320930105842471)
XLA Ops:
  0.7 2.5 %constant_dynamic-slice_fusion = (bf16[2,128,512]{2,1,0:T(8,128)(2,1)S(1)}, bf16[2,128,512]{2,1,0:T(8,128)(2,1)S(1)}, bf16[2,128,512]{2,1,0:T(8,128)(2,1)S(1)}, ...) fusion(bf16[2,128,4096]{2,1,0:T(8,128)(2,1)} %param.24, ...), kind=kLoop, calls=%fused_computation.53 | loop fusion | bytes 4194336 | tf_op jit(solution)/shard_map/dynamic_slice | solution.py:45
  3.2 4.0 %collective-permute-start = (bf16[4,128,512]{2,1,0:T(8,128)(2,1)S(1)}, bf16[4,128,512]{2,1,0:T(8,128)(2,1)S(1)}, u32[]{:S(2)}, u32[]{:S(2)}) collective-permute-start(bf16[4,128,512]{2,1,0:T(8,128)(2,1)S(1)} %pad_maximum_fusion.1), channel_id=1, source_target_pairs={{0,1},{1,0},{2,3},{3,2},{4,5},{5,4},{6,7},{7,6},{8,9},{9,8},{10,11... | collective-permute-start | bytes 1572872 | tf_op jit(solution)/shard_map/ppermute | solution.py:14
  7.3 3.1 %collective-permute-start.1 = (bf16[2,128,512]{2,1,0:T(8,128)(2,1)}, bf16[2,128,512]{2,1,0:T(8,128)(2,1)}, u32[]{:S(2)}, u32[]{:S(2)}) collective-permute-start(bf16[2,128,512]{2,1,0:T(8,128)(2,1)} %get-tuple-element.120), channel_id=1, source_target_pairs={{0,2},{1,3},{2,0},{3,1},{4,6},{5,7},{6,4},{7,5},{8,10},{9,11},{10,... | collective-permute-start | bytes 786440 | tf_op jit(solution)/shard_map/ppermute | solution.py:14
  10.4 1.9 %collective-permute-start.2 = (bf16[2,128,512]{2,1,0:T(8,128)(2,1)S(1)}, bf16[2,128,512]{2,1,0:T(8,128)(2,1)}, u32[]{:S(2)}, u32[]{:S(2)}) collective-permute-start(bf16[2,128,512]{2,1,0:T(8,128)(2,1)S(1)} %get-tuple-element.119), channel_id=1, source_target_pairs={{0,3},{1,2},{2,1},{3,0},{4,7},{5,6},{6,5},{7,4},{8,11},{9,10},{10,... | collective-permute-start | bytes 786440 | tf_op jit(solution)/shard_map/ppermute | solution.py:14
  12.3 4.8 %collective-permute-start.3 = (bf16[2,128,512]{2,1,0:T(8,128)(2,1)S(1)}, bf16[2,128,512]{2,1,0:T(8,128)(2,1)}, u32[]{:S(2)}, u32[]{:S(2)}) collective-permute-start(bf16[2,128,512]{2,1,0:T(8,128)(2,1)S(1)} %get-tuple-element.118), channel_id=1, source_target_pairs={{0,4},{1,5},{2,6},{3,7},{4,0},{5,1},{6,2},{7,3},{8,12},{9,13},{10,... | collective-permute-start | bytes 786440 | tf_op jit(solution)/shard_map/ppermute | solution.py:14
  17.1 3.1 %collective-permute-start.4 = (bf16[2,128,512]{2,1,0:T(8,128)(2,1)S(1)}, bf16[2,128,512]{2,1,0:T(8,128)(2,1)}, u32[]{:S(2)}, u32[]{:S(2)}) collective-permute-start(bf16[2,128,512]{2,1,0:T(8,128)(2,1)S(1)} %get-tuple-element.117), channel_id=1, source_target_pairs={{0,5},{1,4},{2,7},{3,6},{4,1},{5,0},{6,3},{7,2},{8,13},{9,12},{10,... | collective-permute-start | bytes 786440 | tf_op jit(solution)/shard_map/ppermute | solution.py:14
  20.3 17.3 %all-to-all-start = ((bf16[64,8,512]{2,1,0:T(8,128)(2,1)}), bf16[64,8,512]{2,1,0:T(8,128)(2,1)S(1)}, u32[]{:S(2)}, u32[]{:S(2)}) async-start(bf16[64,8,512]{2,1,0:T(8,128)(2,1)} %bitcast.25), calls=%async_computation | async-start | bytes 1048576 | tf_op jit(solution)/shard_map/all_to_all | solution.py:20
  38.4 0.2 scatter.26
  38.6 0.7 constant_dynamic-update-slice_fusion.4
  39.3 4.4 %collective-permute-start.5 = (bf16[2,128,512]{2,1,0:T(8,128)(2,1)S(1)}, bf16[2,128,512]{2,1,0:T(8,128)(2,1)S(1)}, u32[]{:S(2)}, u32[]{:S(2)}) collective-permute-start(bf16[2,128,512]{2,1,0:T(8,128)(2,1)S(1)} %get-tuple-element.123), channel_id=1, source_target_pairs={{0,6},{1,7},{2,4},{3,5},{4,2},{5,3},{6,0},{7,1},{8,14},{9,15},{10,... | collective-permute-start | bytes 786440 | tf_op jit(solution)/shard_map/ppermute | solution.py:14
  43.8 0.0 collective-permute-done.1
  43.8 2.9 %collective-permute-start.6 = (bf16[2,128,512]{2,1,0:T(8,128)(2,1)S(1)}, bf16[2,128,512]{2,1,0:T(8,128)(2,1)S(1)}, u32[]{:S(2)}, u32[]{:S(2)}) collective-permute-start(bf16[2,128,512]{2,1,0:T(8,128)(2,1)S(1)} %get-tuple-element.116), channel_id=1, source_target_pairs={{0,7},{1,6},{2,5},{3,4},{4,3},{5,2},{6,1},{7,0},{8,15},{9,14},{10,... | collective-permute-start | bytes 786440 | tf_op jit(solution)/shard_map/ppermute | solution.py:14
  46.7 1.0 bitcast_dynamic-update-slice_fusion.5
  47.7 0.9 pad_maximum_fusion.2
  48.5 1.9 %collective-permute-start.11 = (bf16[2,2,128,512]{3,2,0,1:T(8,128)(2,1)}, bf16[2,2,128,512]{3,2,0,1:T(8,128)(2,1)}, u32[]{:S(2)}, u32[]{:S(2)}) collective-permute-start(bf16[2,2,128,512]{3,2,0,1:T(8,128)(2,1)} %pad_maximum_fusion.2), channel_id=1, source_target_pairs={{0,2},{2,0},{4,6},{6,4},{1,3},{3,1},{5,7},{7,5},{8,10},{10,8},{12,... | collective-permute-start | bytes 1572872 | tf_op jit(solution)/shard_map/ppermute | solution.py:14
  50.4 1.0 bitcast_dynamic-update-slice_fusion.4
  51.4 0.0 collective-permute-done.3
  51.4 5.6 %collective-permute-start.12 = (bf16[2,2,128,512]{3,2,0,1:T(8,128)(2,1)}, bf16[2,2,128,512]{3,2,0,1:T(8,128)(2,1)}, u32[]{:S(2)}, u32[]{:S(2)}) collective-permute-start(bf16[2,2,128,512]{3,2,0,1:T(8,128)(2,1)} %pad_maximum_fusion.2), channel_id=1, source_target_pairs={{0,4},{2,6},{4,0},{6,2},{1,5},{3,7},{5,1},{7,3},{8,12},{10,14},{12... | collective-permute-start | bytes 1572872 | tf_op jit(solution)/shard_map/ppermute | solution.py:14
  57.0 1.0 bitcast_dynamic-update-slice_fusion.3
  58.0 0.0 collective-permute-done.4
  58.0 2.1 %collective-permute-start.13 = (bf16[2,2,128,512]{3,2,0,1:T(8,128)(2,1)}, bf16[2,2,128,512]{3,2,0,1:T(8,128)(2,1)}, u32[]{:S(2)}, u32[]{:S(2)}) collective-permute-start(bf16[2,2,128,512]{3,2,0,1:T(8,128)(2,1)} %pad_maximum_fusion.2), channel_id=1, source_target_pairs={{0,6},{2,4},{4,2},{6,0},{1,7},{3,5},{5,3},{7,1},{8,14},{10,12},{12... | collective-permute-start | bytes 1572872 | tf_op jit(solution)/shard_map/ppermute | solution.py:14
  60.1 1.0 bitcast_dynamic-update-slice_fusion.2
  61.1 0.0 copy-start.4
  61.2 0.0 copy-start.5
  61.2 0.2 fusion.21
  61.4 0.1 convert_reduce_fusion
  61.5 0.4 copy-done.4
  61.9 0.0 copy-done.5
  61.9 0.6 multiply_subtract_fusion
  62.5 0.9 broadcast_in_dim.7
  63.4 11.9 %all-to-all-start.1 = ((f32[32,8,512]{2,1,0:T(8,128)}), f32[32,8,512]{2,1,0:T(8,128)S(1)}, u32[]{:S(2)}, u32[]{:S(2)}) async-start(f32[32,8,512]{2,1,0:T(8,128)} %broadcast_in_dim.7), calls=%async_computation.1 | async-start | bytes 1048576 | tf_op jit(solution)/shard_map/all_to_all | solution.py:28
  75.3 1.8 %fusion.4 = f32[1024,512]{1,0:T(8,128)S(1)} fusion(bf16[1024,512]{1,0:T(8,128)(2,1)S(1)} %bitcast.109, bf16[1,512,512]{2,1,0:T(8,128)(2,1)} %param.26), kind=kOutput, calls=%fused_computation.14 | convolution fusion | flops 536870912 | bytes 3670016 | tf_op jit(solution)/shard_map/dot_general | solution.py:89
  77.1 0.0 copy-start.2
  77.1 1.2 fusion.19
  78.2 4.4 %collective-permute-start.9 = (f32[2,128,512]{2,1,0:T(8,128)}, f32[2,128,512]{2,1,0:T(8,128)}, u32[]{:S(2)}, u32[]{:S(2)}) collective-permute-start(f32[2,128,512]{2,1,0:T(8,128)} %bitcast.13), channel_id=1, source_target_pairs={{0,6},{2,4},{4,2},{6,0},{1,7},{3,5},{5,3},{7,1},{8,14},{10,12},{12... | collective-permute-start | bytes 1572872 | tf_op jit(solution)/shard_map/ppermute | solution.py:14
  82.6 1.9 %collective-permute-start.8 = (f32[2,128,512]{2,1,0:T(8,128)}, f32[2,128,512]{2,1,0:T(8,128)}, u32[]{:S(2)}, u32[]{:S(2)}) collective-permute-start(f32[2,128,512]{2,1,0:T(8,128)} %bitcast.12), channel_id=1, source_target_pairs={{0,4},{2,6},{4,0},{6,2},{1,5},{3,7},{5,1},{7,3},{8,12},{10,14},{12... | collective-permute-start | bytes 1572872 | tf_op jit(solution)/shard_map/ppermute | solution.py:14
  84.6 0.7 constant_dynamic-update-slice_fusion.3
  85.3 2.7 %collective-permute-start.7 = (f32[2,128,512]{2,1,0:T(8,128)}, f32[2,128,512]{2,1,0:T(8,128)}, u32[]{:S(2)}, u32[]{:S(2)}) collective-permute-start(f32[2,128,512]{2,1,0:T(8,128)} %bitcast.11), channel_id=1, source_target_pairs={{0,2},{2,0},{4,6},{6,4},{1,3},{3,1},{5,7},{7,5},{8,10},{10,8},{12,... | collective-permute-start | bytes 1572872 | tf_op jit(solution)/shard_map/ppermute | solution.py:14
  88.0 1.9 %constant_dynamic-update-slice_fusion.2 = bf16[2,8,128,512]{3,2,0,1:T(8,128)(2,1)} fusion(bf16[2,8,128,512]{3,2,0,1:T(8,128)(2,1)} %constant_dynamic-update-slice_fusion.3, bf16[2,2,128,512]{3,2,0,1:T(8,128)(2,1)} %collective-permute-done.11), kind=kLoop, calls=%fused_computation.50 | loop fusion | bytes 1048576
  89.8 1.9 %constant_dynamic-update-slice_fusion.1 = bf16[2,8,128,512]{3,2,0,1:T(8,128)(2,1)} fusion(bf16[2,8,128,512]{3,2,0,1:T(8,128)(2,1)} %constant_dynamic-update-slice_fusion.2, bf16[2,2,128,512]{3,2,0,1:T(8,128)(2,1)} %collective-permute-done.12), kind=kLoop, calls=%fused_computation.49 | loop fusion | bytes 1048576
  91.7 1.9 %constant_dynamic-update-slice_fusion = bf16[2,8,128,512]{3,2,0,1:T(8,128)(2,1)} fusion(bf16[2,8,128,512]{3,2,0,1:T(8,128)(2,1)} %constant_dynamic-update-slice_fusion.1, bf16[2,2,128,512]{3,2,0,1:T(8,128)(2,1)} %collective-permute-done.13), kind=kLoop, calls=%fused_computation.48 | loop fusion | bytes 1048576 | tf_op jit(solution)/shard_map/concatenate | solution.py:54
  93.6 4.8 %collective-permute-start.14 = (f32[32,8,512]{2,1,0:T(8,128)S(1)}, f32[32,8,512]{2,1,0:T(8,128)S(1)}, u32[]{:S(2)}, u32[]{:S(2)}) collective-permute-start(f32[32,8,512]{2,1,0:T(8,128)S(1)} %all-to-all-done.1), channel_id=1, source_target_pairs={{0,8},{8,0},{1,9},{9,1},{2,10},{10,2},{3,11},{11,3},{4,12},{12,4},... | collective-permute-start | bytes 1572872 | tf_op jit(solution)/shard_map/ppermute | solution.py:14
  98.4 1.7 %fusion.22 = (bf16[1,8,128,512]{3,2,0,1:T(8,128)(2,1)S(1)}, bf16[1,8,128,512]{3,2,0,1:T(8,128)(2,1)S(1)}) fusion(bf16[2,8,128,512]{3,2,0,1:T(8,128)(2,1)} %constant_dynamic-update-slice_fusion), kind=kLoop, calls=%fused_computation.64 | loop fusion | bytes 4194304 | tf_op jit(solution)/shard_map/slice | solution.py:88
  100.1 0.7 fusion.23
  100.9 0.0 copy-start.6
  100.9 0.0 copy-start.7
  100.9 0.1 select_bitcast_fusion.1
  101.0 0.1 pad_maximum_fusion
  101.1 0.8 copy-done.6
  101.9 0.2 copy-done.7
  102.1 4.3 %fusion.7 = (bf16[1,512,512]{2,1,0:T(8,128)(2,1)}, f32[512,512]{1,0:T(8,128)S(1)}) fusion(f32[]{:T(128)} %bitcast.39, f32[512,512]{1,0:T(8,128)S(1)} %fusion.23, bf16[1,512,512]{2,1,0:T(8,128)(2,1)S(1)} %copy-done.6, f32[]{:T(128)} %bitcast.38, bf16[1,512,512]{2,1,0:T(8,128)(2,1)S(1)} %copy-done.7, f32[32,2,8,512]{3,2,1,0:T(8,128)S(1)} %pad_maximum_fusion, ...), kind=kOutput, calls=%fused_computation.21 | convolution fusion | flops 546832384 | bytes 7340048 | tf_op jit(solution)/shard_map/dot_general | solution.py:95
  106.3 0.7 fusion.3
  107.1 0.2 fusion.20
  107.2 4.4 %collective-permute-start.17 = (f32[2,128,512]{2,1,0:T(8,128)S(1)}, f32[2,128,512]{2,1,0:T(8,128)S(1)}, u32[]{:S(2)}, u32[]{:S(2)}) collective-permute-start(f32[2,128,512]{2,1,0:T(8,128)S(1)} %bitcast.120), channel_id=1, source_target_pairs={{0,6},{2,4},{4,2},{6,0},{1,7},{3,5},{5,3},{7,1},{8,14},{10,12},{12... | collective-permute-start | bytes 1572872 | tf_op jit(solution)/shard_map/ppermute | solution.py:14
  111.6 1.9 %collective-permute-start.16 = (f32[2,128,512]{2,1,0:T(8,128)S(1)}, f32[2,128,512]{2,1,0:T(8,128)S(1)}, u32[]{:S(2)}, u32[]{:S(2)}) collective-permute-start(f32[2,128,512]{2,1,0:T(8,128)S(1)} %bitcast.119), channel_id=1, source_target_pairs={{0,4},{2,6},{4,0},{6,2},{1,5},{3,7},{5,1},{7,3},{8,12},{10,14},{12... | collective-permute-start | bytes 1572872 | tf_op jit(solution)/shard_map/ppermute | solution.py:14
  113.6 2.7 %collective-permute-start.15 = (f32[2,128,512]{2,1,0:T(8,128)S(1)}, f32[2,128,512]{2,1,0:T(8,128)S(1)}, u32[]{:S(2)}, u32[]{:S(2)}) collective-permute-start(f32[2,128,512]{2,1,0:T(8,128)S(1)} %bitcast.118), channel_id=1, source_target_pairs={{0,2},{2,0},{4,6},{6,4},{1,3},{3,1},{5,7},{7,5},{8,10},{10,8},{12,... | collective-permute-start | bytes 1572872 | tf_op jit(solution)/shard_map/ppermute | solution.py:14
  116.3 1.6 %add_add_fusion.1 = f32[2,128,512]{2,1,0:T(8,128)S(1)} fusion(f32[2,128,512]{2,1,0:T(8,128)} %collective-permute-done.9, f32[2,128,512]{2,1,0:T(8,128)} %collective-permute-done.8, f32[2,128,512]{2,1,0:T(8,128)S(1)} %bitcast.114, f32[2,128,512]{2,1,0:T(8,128)} %collective-permute-done.7), kind=kLoop, calls=%fused_computation.20 | loop fusion | flops 393216 | bytes 2621440 | tf_op jit(solution)/shard_map/add | solution.py:63
  117.9 2.3 %collective-permute-start.10 = (f32[128,512]{1,0:T(8,128)S(1)}, f32[128,512]{1,0:T(8,128)S(1)}, u32[]{:S(2)}, u32[]{:S(2)}) collective-permute-start(f32[128,512]{1,0:T(8,128)S(1)} %slice_bitcast_fusion.3), channel_id=1, source_target_pairs={{0,1},{1,0},{2,3},{3,2},{4,5},{5,4},{6,7},{7,6},{8,9},{9,8},{10,11... | collective-permute-start | bytes 786440 | tf_op jit(solution)/shard_map/ppermute | solution.py:14
  120.2 14.9 %collective-permute-done.17 = f32[2,128,512]{2,1,0:T(8,128)S(1)} collective-permute-done((f32[2,128,512]{2,1,0:T(8,128)S(1)}, f32[2,128,512]{2,1,0:T(8,128)S(1)}, u32[]{:S(2)}, u32[]{:S(2)}) %collective-permute-start.17) | collective-permute-done | bytes 524320 | tf_op jit(solution)/shard_map/ppermute | solution.py:14
  135.1 2.2 %collective-permute-done.15 = f32[2,128,512]{2,1,0:T(8,128)S(1)} collective-permute-done((f32[2,128,512]{2,1,0:T(8,128)S(1)}, f32[2,128,512]{2,1,0:T(8,128)S(1)}, u32[]{:S(2)}, u32[]{:S(2)}) %collective-permute-start.15) | collective-permute-done | bytes 524320 | tf_op jit(solution)/shard_map/ppermute | solution.py:14
  137.3 0.2 add_add_fusion
  137.6 2.3 %collective-permute-start.18 = (f32[128,512]{1,0:T(8,128)S(1)}, f32[128,512]{1,0:T(8,128)S(1)}, u32[]{:S(2)}, u32[]{:S(2)}) collective-permute-start(f32[128,512]{1,0:T(8,128)S(1)} %slice_bitcast_fusion), channel_id=1, source_target_pairs={{0,1},{1,0},{2,3},{3,2},{4,5},{5,4},{6,7},{7,6},{8,9},{9,8},{10,11... | collective-permute-start | bytes 786440 | tf_op jit(solution)/shard_map/ppermute | solution.py:14
  140.0 6.2 %collective-permute-done.18 = f32[128,512]{1,0:T(8,128)S(1)} collective-permute-done((f32[128,512]{1,0:T(8,128)S(1)}, f32[128,512]{1,0:T(8,128)S(1)}, u32[]{:S(2)}, u32[]{:S(2)}) %collective-permute-start.18) | collective-permute-done | bytes 262176 | tf_op jit(solution)/shard_map/ppermute | solution.py:14
  146.2 0.7 pad_maximum_fusion.3
  (31 shorter events, 0.3 us)
Async XLA Ops:
  0.7 2.5 %copy-start = (bf16[2,128,512]{2,1,0:T(8,128)(2,1)S(1)}, bf16[2,128,512]{2,1,0:T(8,128)(2,1)}, u32[]{:S(2)}) copy-start(bf16[2,128,512]{2,1,0:T(8,128)(2,1)} %param.25) | copy-start | bytes 786436
  3.2 36.1 %collective-permute-start = (bf16[4,128,512]{2,1,0:T(8,128)(2,1)S(1)}, bf16[4,128,512]{2,1,0:T(8,128)(2,1)S(1)}, u32[]{:S(2)}, u32[]{:S(2)}) collective-permute-start(bf16[4,128,512]{2,1,0:T(8,128)(2,1)S(1)} %pad_maximum_fusion.1), channel_id=1, source_target_pairs={{0,1},{1,0},{2,3},{3,2},{4,5},{5,4},{6,7},{7,6},{8,9},{9,8},{10,11... | collective-permute-start | bytes 1572872 | tf_op jit(solution)/shard_map/ppermute | solution.py:14
  7.3 36.5 %collective-permute-start.1 = (bf16[2,128,512]{2,1,0:T(8,128)(2,1)}, bf16[2,128,512]{2,1,0:T(8,128)(2,1)}, u32[]{:S(2)}, u32[]{:S(2)}) collective-permute-start(bf16[2,128,512]{2,1,0:T(8,128)(2,1)} %get-tuple-element.120), channel_id=1, source_target_pairs={{0,2},{1,3},{2,0},{3,1},{4,6},{5,7},{6,4},{7,5},{8,10},{9,11},{10,... | collective-permute-start | bytes 786440 | tf_op jit(solution)/shard_map/ppermute | solution.py:14
  10.4 38.1 %collective-permute-start.2 = (bf16[2,128,512]{2,1,0:T(8,128)(2,1)S(1)}, bf16[2,128,512]{2,1,0:T(8,128)(2,1)}, u32[]{:S(2)}, u32[]{:S(2)}) collective-permute-start(bf16[2,128,512]{2,1,0:T(8,128)(2,1)S(1)} %get-tuple-element.119), channel_id=1, source_target_pairs={{0,3},{1,2},{2,1},{3,0},{4,7},{5,6},{6,5},{7,4},{8,11},{9,10},{10,... | collective-permute-start | bytes 786440 | tf_op jit(solution)/shard_map/ppermute | solution.py:14
  12.3 39.1 %collective-permute-start.3 = (bf16[2,128,512]{2,1,0:T(8,128)(2,1)S(1)}, bf16[2,128,512]{2,1,0:T(8,128)(2,1)}, u32[]{:S(2)}, u32[]{:S(2)}) collective-permute-start(bf16[2,128,512]{2,1,0:T(8,128)(2,1)S(1)} %get-tuple-element.118), channel_id=1, source_target_pairs={{0,4},{1,5},{2,6},{3,7},{4,0},{5,1},{6,2},{7,3},{8,12},{9,13},{10,... | collective-permute-start | bytes 786440 | tf_op jit(solution)/shard_map/ppermute | solution.py:14
  17.1 40.8 %collective-permute-start.4 = (bf16[2,128,512]{2,1,0:T(8,128)(2,1)S(1)}, bf16[2,128,512]{2,1,0:T(8,128)(2,1)}, u32[]{:S(2)}, u32[]{:S(2)}) collective-permute-start(bf16[2,128,512]{2,1,0:T(8,128)(2,1)S(1)} %get-tuple-element.117), channel_id=1, source_target_pairs={{0,5},{1,4},{2,7},{3,6},{4,1},{5,0},{6,3},{7,2},{8,13},{9,12},{10,... | collective-permute-start | bytes 786440 | tf_op jit(solution)/shard_map/ppermute | solution.py:14
  20.3 41.1 %all-to-all-start = ((bf16[64,8,512]{2,1,0:T(8,128)(2,1)}), bf16[64,8,512]{2,1,0:T(8,128)(2,1)S(1)}, u32[]{:S(2)}, u32[]{:S(2)}) async-start(bf16[64,8,512]{2,1,0:T(8,128)(2,1)} %bitcast.25), calls=%async_computation | async-start | bytes 1048576 | tf_op jit(solution)/shard_map/all_to_all | solution.py:20
  39.3 21.7 %copy-start.1 = (bf16[4,128,512]{2,1,0:T(8,128)(2,1)}, bf16[4,128,512]{2,1,0:T(8,128)(2,1)S(1)}, u32[]{:S(2)}) copy-start(bf16[4,128,512]{2,1,0:T(8,128)(2,1)S(1)} %collective-permute-done) | copy-start | bytes 1572868
  39.3 21.7 %collective-permute-start.5 = (bf16[2,128,512]{2,1,0:T(8,128)(2,1)S(1)}, bf16[2,128,512]{2,1,0:T(8,128)(2,1)S(1)}, u32[]{:S(2)}, u32[]{:S(2)}) collective-permute-start(bf16[2,128,512]{2,1,0:T(8,128)(2,1)S(1)} %get-tuple-element.123), channel_id=1, source_target_pairs={{0,6},{1,7},{2,4},{3,5},{4,2},{5,3},{6,0},{7,1},{8,14},{9,15},{10,... | collective-permute-start | bytes 786440 | tf_op jit(solution)/shard_map/ppermute | solution.py:14
  43.8 17.3 %collective-permute-start.6 = (bf16[2,128,512]{2,1,0:T(8,128)(2,1)S(1)}, bf16[2,128,512]{2,1,0:T(8,128)(2,1)S(1)}, u32[]{:S(2)}, u32[]{:S(2)}) collective-permute-start(bf16[2,128,512]{2,1,0:T(8,128)(2,1)S(1)} %get-tuple-element.116), channel_id=1, source_target_pairs={{0,7},{1,6},{2,5},{3,4},{4,3},{5,2},{6,1},{7,0},{8,15},{9,14},{10,... | collective-permute-start | bytes 786440 | tf_op jit(solution)/shard_map/ppermute | solution.py:14
  48.5 36.8 %collective-permute-start.11 = (bf16[2,2,128,512]{3,2,0,1:T(8,128)(2,1)}, bf16[2,2,128,512]{3,2,0,1:T(8,128)(2,1)}, u32[]{:S(2)}, u32[]{:S(2)}) collective-permute-start(bf16[2,2,128,512]{3,2,0,1:T(8,128)(2,1)} %pad_maximum_fusion.2), channel_id=1, source_target_pairs={{0,2},{2,0},{4,6},{6,4},{1,3},{3,1},{5,7},{7,5},{8,10},{10,8},{12,... | collective-permute-start | bytes 1572872 | tf_op jit(solution)/shard_map/ppermute | solution.py:14
  51.4 38.4 %collective-permute-start.12 = (bf16[2,2,128,512]{3,2,0,1:T(8,128)(2,1)}, bf16[2,2,128,512]{3,2,0,1:T(8,128)(2,1)}, u32[]{:S(2)}, u32[]{:S(2)}) collective-permute-start(bf16[2,2,128,512]{3,2,0,1:T(8,128)(2,1)} %pad_maximum_fusion.2), channel_id=1, source_target_pairs={{0,4},{2,6},{4,0},{6,2},{1,5},{3,7},{5,1},{7,3},{8,12},{10,14},{12... | collective-permute-start | bytes 1572872 | tf_op jit(solution)/shard_map/ppermute | solution.py:14
  58.0 33.7 %collective-permute-start.13 = (bf16[2,2,128,512]{3,2,0,1:T(8,128)(2,1)}, bf16[2,2,128,512]{3,2,0,1:T(8,128)(2,1)}, u32[]{:S(2)}, u32[]{:S(2)}) collective-permute-start(bf16[2,2,128,512]{3,2,0,1:T(8,128)(2,1)} %pad_maximum_fusion.2), channel_id=1, source_target_pairs={{0,6},{2,4},{4,2},{6,0},{1,7},{3,5},{5,3},{7,1},{8,14},{10,12},{12... | collective-permute-start | bytes 1572872 | tf_op jit(solution)/shard_map/ppermute | solution.py:14
  61.1 0.7 copy-start.4
  61.2 0.7 copy-start.5
  62.5 14.6 %copy-start.3 = (f32[8,512]{1,0:T(8,128)}, f32[8,512]{1,0:T(8,128)S(1)}, u32[]{:S(2)}) copy-start(f32[8,512]{1,0:T(8,128)S(1)} %get-tuple-element.102) | copy-start | bytes 49156
  63.4 30.2 %all-to-all-start.1 = ((f32[32,8,512]{2,1,0:T(8,128)}), f32[32,8,512]{2,1,0:T(8,128)S(1)}, u32[]{:S(2)}, u32[]{:S(2)}) async-start(f32[32,8,512]{2,1,0:T(8,128)} %broadcast_in_dim.7), calls=%async_computation.1 | async-start | bytes 1048576 | tf_op jit(solution)/shard_map/all_to_all | solution.py:28
  77.1 7.5 %copy-start.2 = (bf16[4,128,512]{2,1,0:T(8,128)(2,1)S(1)}, bf16[4,128,512]{2,1,0:T(8,128)(2,1)}, u32[]{:S(2)}) copy-start(bf16[4,128,512]{2,1,0:T(8,128)(2,1)} %copy-done.1) | copy-start | bytes 1572868
  78.2 35.3 %collective-permute-start.9 = (f32[2,128,512]{2,1,0:T(8,128)}, f32[2,128,512]{2,1,0:T(8,128)}, u32[]{:S(2)}, u32[]{:S(2)}) collective-permute-start(f32[2,128,512]{2,1,0:T(8,128)} %bitcast.13), channel_id=1, source_target_pairs={{0,6},{2,4},{4,2},{6,0},{1,7},{3,5},{5,3},{7,1},{8,14},{10,12},{12... | collective-permute-start | bytes 1572872 | tf_op jit(solution)/shard_map/ppermute | solution.py:14
  82.6 33.6 %collective-permute-start.8 = (f32[2,128,512]{2,1,0:T(8,128)}, f32[2,128,512]{2,1,0:T(8,128)}, u32[]{:S(2)}, u32[]{:S(2)}) collective-permute-start(f32[2,128,512]{2,1,0:T(8,128)} %bitcast.12), channel_id=1, source_target_pairs={{0,4},{2,6},{4,0},{6,2},{1,5},{3,7},{5,1},{7,3},{8,12},{10,14},{12... | collective-permute-start | bytes 1572872 | tf_op jit(solution)/shard_map/ppermute | solution.py:14
  85.3 31.0 %collective-permute-start.7 = (f32[2,128,512]{2,1,0:T(8,128)}, f32[2,128,512]{2,1,0:T(8,128)}, u32[]{:S(2)}, u32[]{:S(2)}) collective-permute-start(f32[2,128,512]{2,1,0:T(8,128)} %bitcast.11), channel_id=1, source_target_pairs={{0,2},{2,0},{4,6},{6,4},{1,3},{3,1},{5,7},{7,5},{8,10},{10,8},{12,... | collective-permute-start | bytes 1572872 | tf_op jit(solution)/shard_map/ppermute | solution.py:14
  93.6 7.3 %collective-permute-start.14 = (f32[32,8,512]{2,1,0:T(8,128)S(1)}, f32[32,8,512]{2,1,0:T(8,128)S(1)}, u32[]{:S(2)}, u32[]{:S(2)}) collective-permute-start(f32[32,8,512]{2,1,0:T(8,128)S(1)} %all-to-all-done.1), channel_id=1, source_target_pairs={{0,8},{8,0},{1,9},{9,1},{2,10},{10,2},{3,11},{11,3},{4,12},{12,4},... | collective-permute-start | bytes 1572872 | tf_op jit(solution)/shard_map/ppermute | solution.py:14
  100.9 1.0 copy-start.6
  100.9 1.2 copy-start.7
  107.2 27.9 %collective-permute-start.17 = (f32[2,128,512]{2,1,0:T(8,128)S(1)}, f32[2,128,512]{2,1,0:T(8,128)S(1)}, u32[]{:S(2)}, u32[]{:S(2)}) collective-permute-start(f32[2,128,512]{2,1,0:T(8,128)S(1)} %bitcast.120), channel_id=1, source_target_pairs={{0,6},{2,4},{4,2},{6,0},{1,7},{3,5},{5,3},{7,1},{8,14},{10,12},{12... | collective-permute-start | bytes 1572872 | tf_op jit(solution)/shard_map/ppermute | solution.py:14
  111.6 23.5 %collective-permute-start.16 = (f32[2,128,512]{2,1,0:T(8,128)S(1)}, f32[2,128,512]{2,1,0:T(8,128)S(1)}, u32[]{:S(2)}, u32[]{:S(2)}) collective-permute-start(f32[2,128,512]{2,1,0:T(8,128)S(1)} %bitcast.119), channel_id=1, source_target_pairs={{0,4},{2,6},{4,0},{6,2},{1,5},{3,7},{5,1},{7,3},{8,12},{10,14},{12... | collective-permute-start | bytes 1572872 | tf_op jit(solution)/shard_map/ppermute | solution.py:14
  113.6 23.8 %collective-permute-start.15 = (f32[2,128,512]{2,1,0:T(8,128)S(1)}, f32[2,128,512]{2,1,0:T(8,128)S(1)}, u32[]{:S(2)}, u32[]{:S(2)}) collective-permute-start(f32[2,128,512]{2,1,0:T(8,128)S(1)} %bitcast.118), channel_id=1, source_target_pairs={{0,2},{2,0},{4,6},{6,4},{1,3},{3,1},{5,7},{7,5},{8,10},{10,8},{12,... | collective-permute-start | bytes 1572872 | tf_op jit(solution)/shard_map/ppermute | solution.py:14
  117.9 22.0 %collective-permute-start.10 = (f32[128,512]{1,0:T(8,128)S(1)}, f32[128,512]{1,0:T(8,128)S(1)}, u32[]{:S(2)}, u32[]{:S(2)}) collective-permute-start(f32[128,512]{1,0:T(8,128)S(1)} %slice_bitcast_fusion.3), channel_id=1, source_target_pairs={{0,1},{1,0},{2,3},{3,2},{4,5},{5,4},{6,7},{7,6},{8,9},{9,8},{10,11... | collective-permute-start | bytes 786440 | tf_op jit(solution)/shard_map/ppermute | solution.py:14
  137.6 8.6 %collective-permute-start.18 = (f32[128,512]{1,0:T(8,128)S(1)}, f32[128,512]{1,0:T(8,128)S(1)}, u32[]{:S(2)}, u32[]{:S(2)}) collective-permute-start(f32[128,512]{1,0:T(8,128)S(1)} %slice_bitcast_fusion), channel_id=1, source_target_pairs={{0,1},{1,0},{2,3},{3,2},{4,5},{5,4},{6,7},{7,6},{8,9},{9,8},{10,11... | collective-permute-start | bytes 786440 | tf_op jit(solution)/shard_map/ppermute | solution.py:14
